TPU v7x, 512 devices: a whole 4x8x8 slice. The times are simulated.
512 devices in a mesh: tm: 8 (over y_lo, x), chan: 64 (over z, y_hi, core).
Axes of the slice: x: 4, y: 8 (y_hi: 4, y_lo: 2; y = y_hi * 2 + y_lo), z: 8, core: 2. Of those that a mesh axis runs over, the one named last changes fastest.
Arguments:
- voltages: int32 [256, 1048576], P('chan', 'tm'), may hold values from 0 to 4095
- beam_weights: int32 [64, 768, 256], P('chan'), may hold values from 0 to 4095
Outputs:
- beam_powers: float32 [8, 768, 8192], P('tm', 'chan')
All inputs are finite; a program needn't handle non-finite values.
Results may differ from a plain program's by a relative error of at most 0.00098.
Values may be sent and summed in bfloat16 or wider, within the bound.
No kernel may reach another device: no remote copies, remote signals or barrier semaphores. Data moves between devices by JAX's collectives and lax.ppermute only.
A program may use at most 128 MiB of HBM per device.

v0:
```python
import math

import jax
import jax.numpy as jnp
from jax import lax
from jax.sharding import PartitionSpec as P

INPUTS = 256
BEAMS = 768
CHANNELS = 8192
SECTION = 128
TAPS = 4
AVERAGE = 16
OUTER = 64


def passed_along(array, axis, by):
    devices = lax.axis_size(axis)
    pairs = [(i, i + by) for i in range(devices) if 0 <= i + by < devices]
    return lax.ppermute(array, axis, pairs)


def unpack_pair(packed):
    real_part = (packed // 64 - 32).astype(jnp.float32)
    imag_part = (packed % 64 - 32).astype(jnp.float32)
    return (real_part, imag_part)


def pfb_taper():
    length = TAPS * CHANNELS
    places = jnp.arange(length, dtype=jnp.int32).astype(jnp.float32)
    offsets = (places - 0.5 * length + 0.5) / CHANNELS
    hann_window = 0.5 - 0.5 * jnp.cos(2.0 * math.pi * (places + 0.5) / length)
    return (jnp.sinc(offsets) * hann_window).reshape(TAPS, CHANNELS)


def stacked_weights(packed):
    real_part, imag_part = unpack_pair(packed)
    upper_rows = jnp.concatenate([real_part, -imag_part], axis=-1)
    lower_rows = jnp.concatenate([imag_part, real_part], axis=-1)
    return jnp.concatenate([upper_rows, lower_rows], axis=-2).astype(jnp.bfloat16)


def phasors(row_count, col_count, length):
    left_index = jnp.arange(row_count, dtype=jnp.int32)
    right_index = jnp.arange(col_count, dtype=jnp.int32)
    turns = left_index[:, None] * right_index[None, :] % length
    angles = turns.astype(jnp.float32) * (-2.0 * math.pi / length)
    return (jnp.cos(angles), jnp.sin(angles))


def block_table(cos_part, sin_part):
    upper_rows = jnp.stack([cos_part, -sin_part])
    lower_rows = jnp.stack([sin_part, cos_part])
    return jnp.stack([upper_rows, lower_rows])


def channelize(stream, spectra_count):
    coeffs = pfb_taper()
    inputs_here = stream.shape[1]
    summed = jnp.zeros((2, inputs_here, spectra_count, CHANNELS), jnp.float32)
    for tap_index in range(TAPS):
        window_piece = lax.slice_in_dim(
            stream, tap_index * CHANNELS, (tap_index + spectra_count) * CHANNELS, axis=2
        )
        summed = (
            summed
            + window_piece.reshape(2, inputs_here, spectra_count, CHANNELS) * coeffs[tap_index]
        )
    frames = summed.reshape(2, inputs_here * spectra_count, OUTER, SECTION)
    outer_cos, outer_sin = phasors(OUTER, OUTER, OUTER)
    twist_cos, twist_sin = phasors(OUTER, SECTION, CHANNELS)
    inner_cos, inner_sin = phasors(SECTION, SECTION, SECTION)
    careful = lax.Precision.HIGH
    first = jnp.einsum(
        "cdpq,dfqn->cfpn", block_table(outer_cos, outer_sin), frames, precision=careful
    )
    turned = jnp.stack(
        [first[0] * twist_cos - first[1] * twist_sin, first[0] * twist_sin + first[1] * twist_cos]
    )
    spectra = jnp.einsum(
        "cdan,dfpn->cfap", block_table(inner_cos, inner_sin), turned, precision=careful
    )
    dft_norm = 1.0 / (32.0 * math.sqrt(CHANNELS))
    spectra = spectra.reshape(2, inputs_here, spectra_count, CHANNELS) * dft_norm
    return jnp.transpose(spectra, (2, 0, 1, 3)).astype(jnp.bfloat16)


def per_device(voltages, beam_weights):
    own_real, own_imag = unpack_pair(voltages)
    own_stream = jnp.stack([own_real, own_imag])
    own_len = voltages.shape[1]
    rim_len = (TAPS - 1) * CHANNELS
    last_frames = own_stream[:, :, own_len - rim_len :].astype(jnp.bfloat16)
    history = passed_along(last_frames, "tm", 1).astype(jnp.float32)
    spectra_here = own_len // CHANNELS
    stream = jnp.concatenate([history, own_stream], axis=2)
    spectra = channelize(stream, spectra_here)
    weight_stack = stacked_weights(beam_weights)
    groups_here = weight_stack.shape[0]
    beam_scale = 1.0 / (24.0 * math.sqrt(INPUTS))
    turned = lax.all_to_all(spectra, "chan", split_axis=3, concat_axis=2, tiled=True)
    item_count = turned.shape[0]
    inputs_all = turned.shape[2]
    chan_width = turned.shape[3]
    merged = turned.reshape(item_count, 2 * inputs_all, groups_here, chan_width // groups_here)

    def one_spectrum(spectrum):
        formed = jnp.einsum(
            "gbi,igc->bgc", weight_stack, spectrum, preferred_element_type=jnp.float32
        )
        beam_real = formed[:BEAMS] * beam_scale
        beam_imag = formed[BEAMS:] * beam_scale
        return (beam_real * beam_real + beam_imag * beam_imag).reshape(BEAMS, chan_width)

    powers = lax.map(one_spectrum, merged)
    mean_count = powers.shape[0] // AVERAGE
    averaged = jnp.mean(powers.reshape(mean_count, AVERAGE, BEAMS, powers.shape[2]), axis=1)
    return lax.all_to_all(averaged, "chan", split_axis=1, concat_axis=2, tiled=True)


def solution(mesh):
    return jax.shard_map(
        per_device,
        mesh=mesh,
        in_specs=(P("chan", "tm"), P("chan", None, None)),
        out_specs=P("tm", "chan", None),
        check_vma=False,
    )
```

profile of v0, /device:TPU:3, one launch (start us, length us, event | category | flops | bytes accessed | tf_op | source)
XLA Modules:
  0.0 293.1 jit_solution(17144350090308309821)
XLA Ops:
  0.0 5.4 %fusion.27 = (f32[4,131072]{1,0:T(4,128)S(1)}, f32[4,131072]{1,0:T(4,128)S(1)}) fusion(s32[4,131072]{1,0:T(4,128)} %param.4), kind=kLoop, calls=%fused_computation.37 | loop fusion | flops 12058624 | bytes 6291456 | tf_op jit(solution)/shard_map/convert_element_type | solution.py:24
  6.7 3.1 %collective-permute-start = (bf16[2,4,24576]{2,1,0:T(4,128)(2,1)S(1)}, bf16[2,4,24576]{2,1,0:T(4,128)(2,1)S(1)}, u32[]{:S(2)}, u32[]{:S(2)}) collective-permute-start(bf16[2,4,24576]{2,1,0:T(4,128)(2,1)S(1)} %fusion.41), channel_id=1, source_target_pairs={{0,64},{64,128},{128,192},{192,256},{256,320},{320,384},{384,448},... | collective-permute-start | bytes 1179656 | tf_op jit(solution)/shard_map/ppermute | solution.py:20
  12.7 2.8 stack.61
  15.5 4.4 %stack.62 = f32[1,64,64,128]{3,2,1,0:T(8,128)} reshape(f32[4,131072]{1,0:T(4,128)} %copy-done) | data formatting | bytes 4194304 | tf_op jit(solution)/shard_map/stack | solution.py:91
  20.0 3.3 %maximum_maximum_fusion = f32[2,4,155648]{2,1,0:T(4,128)S(1)} fusion(f32[1,4,131072]{2,1,0:T(4,128)} %bitcast.91, f32[1,4,131072]{2,1,0:T(4,128)S(1)} %bitcast.89, f32[2,4,24576]{2,1,0:T(4,128)S(1)} %convert_element_type.121), kind=kLoop, calls=%fused_computation.12 | loop fusion | flops 2490368 | bytes 9961472 | tf_op jit(solution)/shard_map/concatenate | solution.py:97
  23.3 4.6 %fusion.90 = (f32[2,4,131072]{2,1,0:T(4,128)}, f32[2,4,131072]{2,1,0:T(4,128)}, f32[2,4,131072]{2,1,0:T(4,128)}) fusion(f32[2,4,155648]{2,1,0:T(4,128)S(1)} %maximum_maximum_fusion), kind=kLoop, calls=%fused_computation.140 | loop fusion | bytes 25165824 | tf_op jit(solution)/shard_map/slice | solution.py:63
  27.9 5.8 %reshape.301 = f32[2,64,64,128]{3,2,1,0:T(8,128)} reshape(f32[2,4,131072]{2,1,0:T(4,128)} %get-tuple-element.52) | data formatting | bytes 8388608 | tf_op jit(solution)/shard_map/reshape | solution.py:68
  33.7 5.8 %reshape.302 = f32[2,64,64,128]{3,2,1,0:T(8,128)} reshape(f32[2,4,131072]{2,1,0:T(4,128)} %get-tuple-element.54) | data formatting | bytes 8388608 | tf_op jit(solution)/shard_map/reshape | solution.py:68
  39.5 5.9 %reshape.303 = f32[2,64,64,128]{3,2,1,0:T(8,128)} reshape(f32[2,4,131072]{2,1,0:T(4,128)} %get-tuple-element.53) | data formatting | bytes 8388608 | tf_op jit(solution)/shard_map/reshape | solution.py:68
  45.5 6.8 %fusion.23 = f32[2,64,64,128]{3,2,0,1:T(8,128)S(1)} fusion(f32[1,64,64,128]{3,2,0,1:T(8,128)} %bitcast.95, f32[1,64,64,128]{3,2,0,1:T(8,128)S(1)} %bitcast.94, f32[2,64,64,128]{3,2,1,0:T(8,128)} %reshape.303, f32[2,64,64,128]{3,2,1,0:T(8,128)} %reshape.302, f32[2,64,64,128]{3,2,1,0:T(8,128)} %reshape.301, f32[64,128]{1,0:T(8,128)S(1)} %get-tuple-element.62, ...), kind=kOutput, calls=%fused_computation.35 | convolution fusion | flops 813711360 | bytes 21168128 | tf_op jit(solution)/shard_map/cdpq,dfqn->cfpn/dot_general | solution.py:75
  52.9 2.1 fusion.35
  55.0 3.2 %copy.42 = bf16[2,64,128,64]{3,2,1,0:T(8,128)(2,1)} copy(bf16[2,64,128,64]{2,3,0,1:T(8,128)(2,1)S(1)} %fusion.35) | data formatting | bytes 4194304 | tf_op jit(solution)/shard_map/convert_element_type | solution.py:86
  58.2 5.7 %convert_element_type.128 = bf16[2,4,16,8192]{3,2,1,0:T(8,128)(2,1)S(1)} reshape(bf16[2,64,128,64]{3,2,1,0:T(8,128)(2,1)} %copy.42) | data formatting | bytes 4194304 | tf_op jit(solution)/shard_map/convert_element_type | solution.py:86
  63.9 16.2 %copy.43 = bf16[16,2,4,8192]{0,2,1,3:T(4,128)(2,1)} copy(bf16[16,2,4,8192]{3,0,2,1:T(8,128)(2,1)S(1)} %bitcast.92) | data formatting | bytes 4194304 | tf_op jit(solution)/shard_map/convert_element_type | solution.py:86
  80.1 20.7 %reshape.311 = bf16[64,2,8192]{2,1,0:T(2,128)(2,1)} reshape(bf16[8192,2,4,16]{3,2,1,0:T(4,128)(2,1)} %bitcast.86) | data formatting | bytes 4194304
  100.8 17.6 %all-to-all-start = ((bf16[64,2,8192]{2,1,0:T(2,128)(2,1)}), bf16[64,2,8192]{2,1,0:T(2,128)(2,1)}, u32[]{:S(2)}, u32[]{:S(2)}) async-start(bf16[64,2,8192]{2,1,0:T(2,128)(2,1)} %reshape.311), calls=%async_computation | async-start | bytes 4194304 | tf_op jit(solution)/shard_map/all_to_all | solution.py:102
  119.7 63.7 %all-to-all-done = bf16[64,2,8192]{2,1,0:T(2,128)(2,1)} async-done(((bf16[64,2,8192]{2,1,0:T(2,128)(2,1)}), bf16[64,2,8192]{2,1,0:T(2,128)(2,1)}, u32[]{:S(2)}, u32[]{:S(2)}) %all-to-all-start) | async-done | bytes 2097184 | tf_op jit(solution)/shard_map/all_to_all | solution.py:102
  183.4 16.5 %reshape.312 = bf16[8192,2,4,16]{3,2,1,0:T(4,128)(2,1)} reshape(bf16[64,2,8192]{2,1,0:T(2,128)(2,1)} %all-to-all-done) | data formatting | bytes 4194304
  199.9 19.1 %copy.54 = bf16[16,2,4,64,128]{4,0,2,3,1:T(8,128)(2,1)} copy(bf16[16,2,4,64,128]{0,2,1,4,3:T(4,128)(2,1)} %bitcast.87) | data formatting | bytes 4194304 | tf_op jit(solution)/shard_map/all_to_all | solution.py:102
  219.0 3.5 %copy.46 = bf16[16,512,1,128]{3,1,2,0:T(8,128)(2,1)} copy(bf16[16,512,1,128]{3,0,1,2:T(8,128)(2,1)} %bitcast.93) | data formatting | bytes 4194304 | tf_op jit(solution)/shard_map/while | solution.py:116
  222.5 38.1 %while.10 = (s32[]{:T(128)}, f32[16,768,128]{1,2,0:T(8,128)}, bf16[16,512,1,128]{3,1,2,0:T(8,128)(2,1)}, bf16[1,1536,512]{2,1,0:T(8,128)(2,1)S(1)}, s32[]{:T(128)}) while((s32[]{:T(128)}, f32[16,768,128]{1,2,0:T(8,128)}, bf16[16,512,1,128]{3,1,2,0:T(8,128)(2,1)}, bf16[1,1536,512]{2,1,0:T(8,128)(2,1)S(1)}, s32[]{:T(128)}) %tuple.35), condition=%wide.region_1.2_spmd, body=%wide.region_0.1_spmd.sunk | while | flops 201818112 | bytes 3671101 | solution.py:116
  248.7 1.6 convolution_bitcast_fusion.2
  260.6 3.2 %reduce_sum.9 = f32[768,128]{0,1:T(8,128)S(1)} reduce(f32[16,768,128]{1,2,0:T(8,128)} %get-tuple-element.27, f32[]{:T(128)} %constant.140.clone.1), dimensions={0}, to_apply=%region_2.3 | reduce | flops 1474560 | bytes 6684676 | tf_op jit(solution)/shard_map/reduce_sum | solution.py:118
  264.1 28.2 %all_to_all.33 = f32[1,768,128]{2,0,1:T(1,128)S(1)} all-to-all(f32[1,768,128]{2,0,1:T(1,128)S(1)} %copy.47), channel_id=1, replica_groups=mesh['tm'=8,'chan'=64] {'chan'}, dimensions={1} | all-to-all | bytes 786432 | tf_op jit(solution)/shard_map/all_to_all | solution.py:119
  (63 shorter events, 43.7 us)
Async XLA Ops:
  5.4 1.3 copy-start
  6.7 13.2 %collective-permute-start = (bf16[2,4,24576]{2,1,0:T(4,128)(2,1)S(1)}, bf16[2,4,24576]{2,1,0:T(4,128)(2,1)S(1)}, u32[]{:S(2)}, u32[]{:S(2)}) collective-permute-start(bf16[2,4,24576]{2,1,0:T(4,128)(2,1)S(1)} %fusion.41), channel_id=1, source_target_pairs={{0,64},{64,128},{128,192},{192,256},{256,320},{320,384},{384,448},... | collective-permute-start | bytes 1179656 | tf_op jit(solution)/shard_map/ppermute | solution.py:20
  39.5 5.9 %copy-start.1 = (f32[1,64,64,128]{3,2,1,0:T(8,128)S(1)}, f32[1,64,64,128]{3,2,1,0:T(8,128)}, u32[]{:S(2)}) copy-start(f32[1,64,64,128]{3,2,1,0:T(8,128)} %stack.61) | copy-start | bytes 6291460
  39.5 5.9 %copy-start.3 = (f32[1,2,64,64]{3,2,1,0:T(8,128)S(1)}, f32[1,2,64,64]{3,2,1,0:T(8,128)}, u32[]{:S(2)}) copy-start(f32[1,2,64,64]{3,2,1,0:T(8,128)} %get-tuple-element.68) | copy-start | bytes 98308
  45.5 6.8 %copy-start.4 = (f32[64,128]{1,0:T(8,128)S(1)}, f32[64,128]{1,0:T(8,128)}, u32[]{:S(2)}) copy-start(f32[64,128]{1,0:T(8,128)} %get-tuple-element.71) | copy-start | bytes 98308
  45.5 6.8 %copy-start.5 = (f32[64,128]{1,0:T(8,128)S(1)}, f32[64,128]{1,0:T(8,128)}, u32[]{:S(2)}) copy-start(f32[64,128]{1,0:T(8,128)} %get-tuple-element.72) | copy-start | bytes 98308
  100.8 17.6 %copy-start.2 = (s32[1,768,256]{2,1,0:T(8,128)S(1)}, s32[1,768,256]{2,1,0:T(8,128)}, u32[]{:S(2)}) copy-start(s32[1,768,256]{2,1,0:T(8,128)} %param.5) | copy-start | bytes 2359300
  100.8 82.6 %all-to-all-start = ((bf16[64,2,8192]{2,1,0:T(2,128)(2,1)}), bf16[64,2,8192]{2,1,0:T(2,128)(2,1)}, u32[]{:S(2)}, u32[]{:S(2)}) async-start(bf16[64,2,8192]{2,1,0:T(2,128)(2,1)} %reshape.311), calls=%async_computation | async-start | bytes 4194304 | tf_op jit(solution)/shard_map/all_to_all | solution.py:102
where the time goes:
time: 295 us; the launch traced here: 293 us
  local copies, waits for them, and re-layouts  116 us (39%)
  waiting for transfers between devices  63.7 us (22%)
  matrix products  33.7 us (11%)
  other arithmetic  30 us (10%)
  blocking collectives  28.2 us (10%)
  starting transfers between devices  20.7 us (7%)
    all_to_all x1, waiting for transfers between devices, per_device(): lax.all_to_all(spectra, 'chan', split_axis=3, concat_axis=2, tiled=True)  63.7 us
    unnamed x14, local copies, waits for them, and re-layouts  38.3 us
    all_to_all x1, blocking collectives, per_device(): lax.all_to_all(averaged, 'chan', split_axis=1, concat_axis=2, tiled=True)  28.2 us
    convert_element_type x3, local copies, waits for them, and re-layouts, channelize(): return jnp.transpose(spectra, (2, 0, 1, 3)).astype(jnp.bfloat16)  25 us
    dot_general x16, matrix products, one_spectrum(): jnp.einsum('gbi,igc->bgc', weight_stack, spectrum, preferred_element_type...  24.8 us
    all_to_all x1, local copies, waits for them, and re-layouts, per_device(): lax.all_to_all(spectra, 'chan', split_axis=3, concat_axis=2, tiled=True)  19.1 us
    all_to_all x1, starting transfers between devices, per_device(): lax.all_to_all(spectra, 'chan', split_axis=3, concat_axis=2, tiled=True)  17.6 us
    reshape x3, local copies, waits for them, and re-layouts, channelize(): window_piece.reshape(2, inputs_here, spectra_count, CHANNELS)  17.6 us
  transfers between devices with their start and end apart: 2, of which 1 were waited for; matrix products, arithmetic and copies ran while one was open for 4% of the time, Pallas kernels for 0%

commit v1 on v0

v1 whole, which is shorter than its diff:
```python
import functools
import math

import jax
import jax.numpy as jnp
import numpy as np
from jax import lax
from jax.experimental import pallas as pl
from jax.experimental.pallas import tpu as pltpu
from jax.sharding import PartitionSpec as P

INPUTS = 256
BEAMS = 768
CHANNELS = 8192
SECTION = 128
TAPS = 4
AVERAGE = 16
OUTER = 64
GROUPS = 64
ZERO_SAMPLE = 32 * 64 + 32
VMEM_BYTES = 48 * 1024 * 1024

INPUTS_HERE = 4
FRAME_ROWS = OUTER * INPUTS_HERE
PAIR_ROWS = 16


def split_table(table):
    high = table.astype(jnp.bfloat16)
    low = (table - np.asarray(high, np.float64)).astype(jnp.bfloat16)
    return np.asarray(high), np.asarray(low)


def pfb_taper():
    places = np.arange(TAPS * CHANNELS, dtype=np.float64)
    length = TAPS * CHANNELS
    offsets = (places - 0.5 * length + 0.5) / CHANNELS
    hann_window = 0.5 - 0.5 * np.cos(2.0 * math.pi * (places + 0.5) / length)
    taper = np.sinc(offsets) * hann_window
    return taper.astype(np.float32).reshape(TAPS, OUTER, SECTION)


def phasors(left_index, right_index, length):
    turns = np.outer(left_index, right_index) % length
    angles = turns * (-2.0 * math.pi / length)
    return np.cos(angles), np.sin(angles)


def outer_table():
    cos_part, sin_part = phasors(np.arange(OUTER), np.arange(OUTER), OUTER)
    table = np.zeros((2, 2, OUTER, 2, 2, OUTER))
    for f in range(2):
        table[0, f, :, f, 0, :] = cos_part
        table[0, f, :, f, 1, :] = -sin_part
        table[1, f, :, f, 0, :] = sin_part
        table[1, f, :, f, 1, :] = cos_part
    return table.reshape(4 * OUTER, 4 * OUTER)


def twist_table():
    norm = 1.0 / (32.0 * math.sqrt(CHANNELS))
    cos_part, sin_part = phasors(np.arange(OUTER), np.arange(SECTION), CHANNELS)
    return (
        np.tile(cos_part * norm, (2, 1)).astype(np.float32),
        np.tile(sin_part * norm, (2, 1)).astype(np.float32),
    )


def inner_table():
    channel = np.arange(SECTION).reshape(GROUPS, 2).T
    table = np.zeros((2, 2, GROUPS, 2, SECTION))
    for half in range(2):
        cos_part, sin_part = phasors(channel[half], np.arange(SECTION), SECTION)
        table[half, 0, :, 0, :] = cos_part
        table[half, 0, :, 1, :] = -sin_part
        table[half, 1, :, 0, :] = sin_part
        table[half, 1, :, 1, :] = cos_part
    return table.reshape(4 * GROUPS, 2 * SECTION)


def two_halves(values):
    high = values.astype(jnp.bfloat16)
    low = (values - high.astype(jnp.float32)).astype(jnp.bfloat16)
    return high, low


def careful_dot(left_high, left_low, right, contract):
    right_high, right_low = two_halves(right)
    dims = (contract, ((), ()))

    def dot(left, values):
        return lax.dot_general(left, values, dims, preferred_element_type=jnp.float32)

    return dot(left_high, right_high) + (dot(left_high, right_low) + dot(left_low, right_high))


def channelize_kernel(
    frame0, frame1, frame2, frame3, frame4, taper,
    outer_high, outer_low, twist_cos, twist_sin, inner_high, inner_low,
    out, strided,
):
    packed_frames = (frame0, frame1, frame2, frame3, frame4)
    columns = []
    for i in range(INPUTS_HERE):
        summed = {}
        for t, packed_ref in enumerate(packed_frames):
            packed = packed_ref[pl.ds(i, OUTER, stride=INPUTS_HERE), :]
            parts = (
                ((packed >> 6) - 32).astype(jnp.float32),
                ((packed & 63) - 32).astype(jnp.float32),
            )
            for f in range(2):
                if 0 <= t - f < TAPS:
                    for part in range(2):
                        term = parts[part] * taper[t - f]
                        key = (f, part)
                        summed[key] = summed[key] + term if key in summed else term
        columns.append(
            jnp.concatenate([summed[f, part] for f in range(2) for part in range(2)], axis=0)
        )
    frames = jnp.concatenate(columns, axis=1)
    first = careful_dot(outer_high[...], outer_low[...], frames, ((1,), (0,)))
    cos_part, sin_part = twist_cos[...], twist_sin[...]
    turned = []
    for i in range(INPUTS_HERE):
        real_part = first[:SECTION, i * SECTION : (i + 1) * SECTION]
        imag_part = first[SECTION:, i * SECTION : (i + 1) * SECTION]
        turned.append(
            jnp.concatenate(
                [
                    real_part * cos_part - imag_part * sin_part,
                    real_part * sin_part + imag_part * cos_part,
                ],
                axis=1,
            )
        )
    turned = jnp.concatenate(turned, axis=0)
    spectra = careful_dot(inner_high[...], inner_low[...], turned, ((1,), (1,)))
    for half in range(2):
        for part in range(2):
            top = (half * 2 + part) * GROUPS
            for i in range(INPUTS_HERE):
                row = half * 8 + i * 2 + part
                strided[pl.ds(row, GROUPS, stride=PAIR_ROWS), :] = spectra[
                    top : top + GROUPS, i * SECTION : (i + 1) * SECTION
                ]
    out[...] = strided[...].astype(jnp.bfloat16).reshape(out.shape)


def channelize(packed_rows, first_frame, pairs):
    outer_high, outer_low = split_table(outer_table())
    inner_high, inner_low = split_table(inner_table())
    twist_cos, twist_sin = twist_table()
    tables = (pfb_taper(), outer_high, outer_low, twist_cos, twist_sin, inner_high, inner_low)

    def frame_spec(t):
        return pl.BlockSpec((FRAME_ROWS, SECTION), lambda pair: (first_frame + 2 * pair + t, 0))

    def whole(table):
        return pl.BlockSpec(table.shape, lambda pair: (0,) * table.ndim)

    return pl.pallas_call(
        channelize_kernel,
        grid=(pairs,),
        in_specs=[frame_spec(t) for t in range(5)] + [whole(table) for table in tables],
        out_specs=pl.BlockSpec((GROUPS, 1, PAIR_ROWS, SECTION), lambda pair: (0, pair, 0, 0)),
        out_shape=jax.ShapeDtypeStruct((GROUPS, pairs, PAIR_ROWS, SECTION), jnp.bfloat16),
        scratch_shapes=[pltpu.VMEM((GROUPS * PAIR_ROWS, SECTION), jnp.float32)],
        compiler_params=pltpu.CompilerParams(vmem_limit_bytes=VMEM_BYTES),
        cost_estimate=pl.CostEstimate(
            flops=pairs * 3 * 2 * 2 * 256 * 256 * 512,
            bytes_accessed=pairs * (5 * 131072 + 262144),
            transcendentals=0,
        ),
        name="channelize",
    )(*([packed_rows] * 5), *(jnp.asarray(table) for table in tables))


def spread_tables():
    even = np.zeros((INPUTS, INPUTS, 2))
    odd = np.zeros((INPUTS, INPUTS, 2))
    even[np.arange(INPUTS), np.arange(INPUTS), 0] = 1.0
    odd[np.arange(INPUTS), np.arange(INPUTS), 1] = 1.0
    even = even.reshape(INPUTS, 2 * INPUTS)
    odd = odd.reshape(INPUTS, 2 * INPUTS)
    upper = np.concatenate([even, -odd], axis=0)
    lower = np.concatenate([odd, even], axis=0)
    return upper.astype(jnp.bfloat16), lower.astype(jnp.bfloat16)


def weights_kernel(packed_ref, upper, lower, out):
    packed = packed_ref[...]
    parts = jnp.concatenate(
        [
            ((packed >> 6) - 32).astype(jnp.float32).astype(jnp.bfloat16),
            ((packed & 63) - 32).astype(jnp.float32).astype(jnp.bfloat16),
        ],
        axis=1,
    )
    out[:BEAMS] = jnp.dot(parts, upper[...], preferred_element_type=jnp.float32).astype(
        jnp.bfloat16
    )
    out[BEAMS:] = jnp.dot(parts, lower[...], preferred_element_type=jnp.float32).astype(
        jnp.bfloat16
    )


def stacked_weights(packed):
    upper, lower = spread_tables()
    return pl.pallas_call(
        weights_kernel,
        out_shape=jax.ShapeDtypeStruct((2 * BEAMS, 2 * INPUTS), jnp.bfloat16),
        in_specs=[pl.BlockSpec(memory_space=pltpu.VMEM)] * 3,
        out_specs=pl.BlockSpec(memory_space=pltpu.VMEM),
        compiler_params=pltpu.CompilerParams(vmem_limit_bytes=VMEM_BYTES),
        cost_estimate=pl.CostEstimate(
            flops=2 * 2 * BEAMS * 512 * 512, bytes_accessed=5 * 2**20, transcendentals=0
        ),
        name="stack_weights",
    )(packed, jnp.asarray(upper), jnp.asarray(lower))


def beam_block(weights_ref, spectra_ref):
    spectra = spectra_ref[...].astype(jnp.float32).reshape(GROUPS, PAIR_ROWS, SECTION)
    paired = jnp.concatenate(
        [
            spectra[:, half * 8 : half * 8 + 8].reshape(2 * INPUTS, SECTION).astype(jnp.bfloat16)
            for half in range(2)
        ],
        axis=1,
    )
    formed = jnp.dot(weights_ref[...], paired, preferred_element_type=jnp.float32)
    real_part, imag_part = formed[:BEAMS], formed[BEAMS:]
    return real_part * real_part + imag_part * imag_part


def start_kernel(weights_ref, spectra_ref, out):
    powers = beam_block(weights_ref, spectra_ref)

    @pl.when(pl.program_id(0) == 0)
    def _():
        out[...] = powers

    @pl.when(pl.program_id(0) > 0)
    def _():
        out[...] += powers


def finish_kernel(weights_ref, spectra_ref, before, out, total):
    powers = beam_block(weights_ref, spectra_ref)

    @pl.when(pl.program_id(0) == 0)
    def _():
        total[...] = before[...] + powers

    @pl.when(pl.program_id(0) > 0)
    def _():
        total[...] += powers

    @pl.when(pl.program_id(0) == pl.num_programs(0) - 1)
    def _():
        scale = 1.0 / (24.0 * math.sqrt(INPUTS)) ** 2 / AVERAGE
        sums = []
        for half in range(2):
            part = total[:, half * SECTION : (half + 1) * SECTION]
            sums.append((part + pltpu.roll(part, OUTER, 1)) * scale)
        lane = lax.broadcasted_iota(jnp.int32, (BEAMS, SECTION), 1)
        out[...] = jnp.where(lane < OUTER, sums[0], sums[1])


def beam_call(weights, spectra, before=None):
    pairs = spectra.shape[1]
    in_specs = [
        pl.BlockSpec((2 * BEAMS, 2 * INPUTS), lambda pair: (0, 0)),
        pl.BlockSpec((GROUPS, 1, PAIR_ROWS, SECTION), lambda pair: (0, pair, 0, 0)),
    ]
    operands = [weights, spectra]
    width = 2 * SECTION
    scratch = []
    if before is not None:
        in_specs.append(pl.BlockSpec((BEAMS, width), lambda pair: (0, 0)))
        operands.append(before)
        scratch.append(pltpu.VMEM((BEAMS, width), jnp.float32))
        width = SECTION
    return pl.pallas_call(
        start_kernel if before is None else finish_kernel,
        grid=(pairs,),
        in_specs=in_specs,
        out_specs=pl.BlockSpec((BEAMS, width), lambda pair: (0, 0)),
        out_shape=jax.ShapeDtypeStruct((BEAMS, width), jnp.float32),
        scratch_shapes=scratch,
        compiler_params=pltpu.CompilerParams(vmem_limit_bytes=VMEM_BYTES),
        cost_estimate=pl.CostEstimate(
            flops=pairs * 2 * 1536 * 512 * 256,
            bytes_accessed=1536 * 512 * 2 + pairs * 262144 + 3 * 768 * 256 * 4,
            transcendentals=0,
        ),
        name="beams_start" if before is None else "beams_finish",
    )(*operands)


LATE_PAIRS = 4


def per_device(voltages, beam_weights):
    inputs_here, own_len = voltages.shape
    spectra_here = own_len // CHANNELS
    rows = jnp.transpose(voltages.reshape(inputs_here, own_len // SECTION, SECTION), (1, 0, 2))
    rows = rows.reshape(own_len // SECTION * inputs_here, SECTION)
    rim = (TAPS - 1) * FRAME_ROWS
    devices = lax.axis_size("tm")
    history = lax.ppermute(
        rows[rows.shape[0] - rim :] - ZERO_SAMPLE,
        "tm",
        [(i, i + 1) for i in range(devices - 1)],
    )
    late = 2 * LATE_PAIRS
    late_spectra = channelize(rows, spectra_here - late - 3, LATE_PAIRS)
    late_turned = lax.all_to_all(late_spectra, "chan", 0, 0, tiled=True)
    early = spectra_here - late
    early_rows = jnp.concatenate([history + ZERO_SAMPLE, rows[: early * FRAME_ROWS]], axis=0)
    early_spectra = channelize(early_rows, 0, early // 2)
    early_turned = lax.all_to_all(early_spectra, "chan", 0, 0, tiled=True)
    weights = stacked_weights(beam_weights[0])
    powers = beam_call(weights, late_turned)
    averaged = beam_call(weights, early_turned, powers)
    return lax.all_to_all(averaged[None], "chan", split_axis=1, concat_axis=2, tiled=True)


def solution(mesh):
    return jax.shard_map(
        per_device,
        mesh=mesh,
        in_specs=(P("chan", "tm"), P("chan", None, None)),
        out_specs=P("tm", "chan", None),
        check_vma=False,
    )
```

time: 295 us -> 147 us (0.50)
  the two profiles are of different devices: /device:TPU:3 before, /device:TPU:9 now
where the time goes in v1:
time: 147 us; the launch traced here: 146 us
  waiting for transfers between devices  53.1 us (36%)
  starting transfers between devices  31.8 us (22%)
  blocking collectives  28.4 us (19%)
  Pallas kernels  18.6 us (13%)
  local copies, waits for them, and re-layouts  13.8 us (9%)
    ppermute x1, waiting for transfers between devices, per_device(): lax.ppermute(rows[rows.shape[0] - rim:] - ZERO_SAMPLE, 'tm', [(i, i + 1)...  31.6 us
    all_to_all x1, blocking collectives, per_device(): lax.all_to_all(averaged[None], 'chan', split_axis=1, concat_axis=2, tiled...  28.4 us
    all_to_all x1, waiting for transfers between devices, per_device(): early_turned = lax.all_to_all(early_spectra, 'chan', 0, 0, tiled=True)  21.6 us
    all_to_all x1, starting transfers between devices, per_device(): late_turned = lax.all_to_all(late_spectra, 'chan', 0, 0, tiled=True)  16 us
    unnamed x42, local copies, waits for them, and re-layouts  13 us
    all_to_all x1, starting transfers between devices, per_device(): early_turned = lax.all_to_all(early_spectra, 'chan', 0, 0, tiled=True)  12.7 us
    pallas_call x2, Pallas kernels, channelize(): pl.pallas_call(channelize_kernel, grid=(pairs,), in_specs=[frame_spec(t)...  10.7 us
    pallas_call x2, Pallas kernels, beam_call(): pl.pallas_call(start_kernel if before is None else finish_kernel, grid=(p...  6.95 us
  transfers between devices with their start and end apart: 3, of which 2 were waited for; matrix products, arithmetic and copies ran while one was open for 0% of the time, Pallas kernels for 6%

profile of v1, /device:TPU:9, one launch (start us, length us, event | category | flops | bytes accessed | tf_op | source)
XLA Modules:
  0.0 146.2 jit_solution(6041891032496407661)
XLA Ops:
  0.0 1.6 %copy-done = s32[4,131072]{1,0:T(4,128)S(1)} copy-done((s32[4,131072]{1,0:T(4,128)S(1)}, s32[4,131072]{1,0:T(4,128)}, u32[]{:S(2)}) %copy-start) | copy-done | bytes 2097176
  1.6 0.9 copy-done.3
  2.5 0.9 copy-done.5
  3.4 0.9 copy-done.7
  4.3 0.9 copy-done.9
  5.2 0.9 copy-done.11
  6.1 0.8 copy-done.15
  7.0 0.8 copy-done.17
  7.8 5.3 %channelize.3 = bf16[64,4,16,128]{3,2,1,0:T(8,128)(2,1)} custom-call(s32[4096,128]{1,0:T(8,128)S(1)} %bitcast.15, s32[4096,128]{1,0:T(8,128)S(1)} %bitcast.16, s32[4096,128]{1,0:T(8,128)S(1)} %bitcast.17, s32[4096,128]{1,0:T(8,128)S(1)} %bitcast.18, s32[4096,128]{1,0:T(8,128)S(1)} %bitcast.19, f32[4,64,128]{2,1,0:T(8,128)S(1)} %copy-done.11, ...), custom_call_target="tpu_custom_call" | custom-call | flops 1610612736 | bytes 3670016 | tf_op jit(solution)/shard_map/channelize/pallas_call | solution.py:162
  13.1 16.0 %all-to-all-start.1 = ((bf16[64,4,16,128]{3,2,1,0:T(8,128)(2,1)}), bf16[64,4,16,128]{3,2,1,0:T(8,128)(2,1)S(1)}, u32[]{:S(2)}, u32[]{:S(2)}) async-start(bf16[64,4,16,128]{3,2,1,0:T(8,128)(2,1)} %channelize.3), calls=%async_computation.1 | async-start | bytes 2097152 | tf_op jit(solution)/shard_map/all_to_all | solution.py:319
  29.3 3.1 %collective-permute-start = (s32[768,128]{1,0:T(8,128)S(1)}, s32[768,128]{1,0:T(8,128)S(1)}, u32[]{:S(2)}, u32[]{:S(2)}) collective-permute-start(s32[768,128]{1,0:T(8,128)S(1)} %bitcast.26), channel_id=1, source_target_pairs={{0,64},{64,128},{128,192},{192,256},{256,320},{320,384},{384,448},... | collective-permute-start | bytes 1179656 | tf_op jit(solution)/shard_map/ppermute | solution.py:312
  32.5 31.6 %collective-permute-done = s32[768,128]{1,0:T(8,128)S(1)} collective-permute-done((s32[768,128]{1,0:T(8,128)S(1)}, s32[768,128]{1,0:T(8,128)S(1)}, u32[]{:S(2)}, u32[]{:S(2)}) %collective-permute-start) | collective-permute-done | bytes 393248 | tf_op jit(solution)/shard_map/ppermute | solution.py:312
  65.3 5.4 %channelize.2 = bf16[64,4,16,128]{3,2,1,0:T(8,128)(2,1)} custom-call(s32[2816,128]{1,0:T(8,128)S(1)} %pad_add_fusion.frame0.frame1.frame2.frame3.frame4, s32[2816,128]{1,0:T(8,128)S(1)} %pad_add_fusion.frame0.frame1.frame2.frame3.frame4, s32[2816,128]{1,0:T(8,128)S(1)} %pad_add_fusion.frame0.frame1.frame2.frame3.frame4, ...), custom_call_target="tpu_custom_call" | custom-call | flops 1610612736 | bytes 3670016 | tf_op jit(solution)/shard_map/channelize/pallas_call | solution.py:162
  70.6 12.7 %all-to-all-start = ((bf16[64,4,16,128]{3,2,1,0:T(8,128)(2,1)}), bf16[64,4,16,128]{3,2,1,0:T(8,128)(2,1)}, u32[]{:S(2)}, u32[]{:S(2)}) async-start(bf16[64,4,16,128]{3,2,1,0:T(8,128)(2,1)} %channelize.2), calls=%async_computation | async-start | bytes 2097152 | tf_op jit(solution)/shard_map/all_to_all | solution.py:323
  83.3 1.1 copy-done.2
  84.4 1.0 copy-done.14
  85.5 1.0 stack_weights.1.weights_ref
  86.5 2.8 %beams_start.1.before = f32[768,256]{1,0:T(8,128)S(1)} custom-call(bf16[1536,512]{1,0:T(8,128)(2,1)S(1)} %stack_weights.1.weights_ref, bf16[64,4,16,128]{3,2,1,0:T(8,128)(2,1)S(1)} %all-to-all-done.1.spectra_ref), custom_call_target="tpu_custom_call" | custom-call | flops 1610612736 | bytes 4980736 | tf_op jit(solution)/shard_map/beams_start/pallas_call | solution.py:285
  89.2 0.9 copy-done.19
  90.1 21.6 %all-to-all-done.spectra_ref = bf16[64,4,16,128]{3,2,1,0:T(8,128)(2,1)} async-done(((bf16[64,4,16,128]{3,2,1,0:T(8,128)(2,1)}), bf16[64,4,16,128]{3,2,1,0:T(8,128)(2,1)}, u32[]{:S(2)}, u32[]{:S(2)}) %all-to-all-start) | async-done | bytes 1048608 | tf_op jit(solution)/shard_map/all_to_all | solution.py:323
  111.7 1.1 copy-done.20
  112.8 4.2 %beams_finish.1 = f32[768,128]{1,0:T(8,128)S(1)} custom-call(bf16[1536,512]{1,0:T(8,128)(2,1)S(1)} %stack_weights.1.weights_ref, bf16[64,4,16,128]{3,2,1,0:T(8,128)(2,1)} %all-to-all-done.spectra_ref, f32[768,256]{1,0:T(8,128)S(1)} %copy-done.20), custom_call_target="tpu_custom_call" | custom-call | flops 1610612736 | bytes 4980736 | tf_op jit(solution)/shard_map/beams_finish/pallas_call | solution.py:285
  117.0 28.4 %all_to_all.28 = f32[1,768,128]{2,0,1:T(1,128)S(1)} all-to-all(f32[1,768,128]{2,0,1:T(1,128)S(1)} %bitcast.23), channel_id=1, replica_groups=mesh['tm'=8,'chan'=64] {'chan'}, dimensions={1} | all-to-all | bytes 786432 | tf_op jit(solution)/shard_map/all_to_all | solution.py:327
  145.5 0.8 copy.26
  (35 shorter events, 1.3 us)
Async XLA Ops:
  0.0 1.6 %copy-start = (s32[4,131072]{1,0:T(4,128)S(1)}, s32[4,131072]{1,0:T(4,128)}, u32[]{:S(2)}) copy-start(s32[4,131072]{1,0:T(4,128)} %param.18) | copy-start | bytes 6291460
  1.6 0.9 copy-start.3
  2.5 0.9 copy-start.5
  3.4 0.9 copy-start.7
  4.3 0.9 copy-start.9
  5.2 0.9 copy-start.11
  6.1 0.8 copy-start.15
  7.0 0.8 copy-start.17
  13.1 16.1 %copy-start.1 = (s32[4,131072]{1,0:T(4,128)S(1)}, s32[4,131072]{1,0:T(4,128)}, u32[]{:S(2)}) copy-start(s32[4,131072]{1,0:T(4,128)} %param.18) | copy-start | bytes 6291460
  13.1 57.5 %all-to-all-start.1 = ((bf16[64,4,16,128]{3,2,1,0:T(8,128)(2,1)}), bf16[64,4,16,128]{3,2,1,0:T(8,128)(2,1)S(1)}, u32[]{:S(2)}, u32[]{:S(2)}) async-start(bf16[64,4,16,128]{3,2,1,0:T(8,128)(2,1)} %channelize.3), calls=%async_computation.1 | async-start | bytes 2097152 | tf_op jit(solution)/shard_map/all_to_all | solution.py:319
  29.3 34.8 %collective-permute-start = (s32[768,128]{1,0:T(8,128)S(1)}, s32[768,128]{1,0:T(8,128)S(1)}, u32[]{:S(2)}, u32[]{:S(2)}) collective-permute-start(s32[768,128]{1,0:T(8,128)S(1)} %bitcast.26), channel_id=1, source_target_pairs={{0,64},{64,128},{128,192},{192,256},{256,320},{320,384},{384,448},... | collective-permute-start | bytes 1179656 | tf_op jit(solution)/shard_map/ppermute | solution.py:312
  64.1 0.9 copy-start.4
  64.1 1.0 copy-start.6
  64.1 1.0 copy-start.8
  64.1 1.1 copy-start.10
  64.1 1.1 copy-start.12
  64.1 1.1 copy-start.16
  64.1 1.1 copy-start.18
  70.6 12.7 %copy-start.13 = (bf16[512,512]{1,0:T(8,128)(2,1)S(1)}, bf16[512,512]{1,0:T(8,128)(2,1)}, u32[]{:S(2)}) copy-start(bf16[512,512]{1,0:T(8,128)(2,1)} %constant.30.clone.lower) | copy-start | bytes 1572868
  70.6 41.1 %all-to-all-start = ((bf16[64,4,16,128]{3,2,1,0:T(8,128)(2,1)}), bf16[64,4,16,128]{3,2,1,0:T(8,128)(2,1)}, u32[]{:S(2)}, u32[]{:S(2)}) async-start(bf16[64,4,16,128]{3,2,1,0:T(8,128)(2,1)} %channelize.2), calls=%async_computation | async-start | bytes 2097152 | tf_op jit(solution)/shard_map/all_to_all | solution.py:323
  83.3 1.1 copy-start.2
  84.4 1.0 copy-start.14
  89.2 0.9 copy-start.19
  111.7 1.1 copy-start.20

commit v2 on v1

--- a/solution.py
+++ b/solution.py
@@ -18,7 +18,8 @@
 OUTER = 64
 GROUPS = 64
 ZERO_SAMPLE = 32 * 64 + 32
-VMEM_BYTES = 48 * 1024 * 1024
+VMEM_BYTES = 60 * 1024 * 1024
+BEAM_VMEM_BYTES = 32 * 1024 * 1024
 
 INPUTS_HERE = 4
 FRAME_ROWS = OUTER * INPUTS_HERE
@@ -147,7 +148,11 @@
     out[...] = strided[...].astype(jnp.bfloat16).reshape(out.shape)
 
 
-def channelize(packed_rows, first_frame, pairs):
+def channelize_more_kernel(*refs):
+    channelize_kernel(*refs[:12], *refs[13:])
+
+
+def channelize(packed_rows, first_frame, pairs, first_pair, all_pairs, into=None):
     outer_high, outer_low = split_table(outer_table())
     inner_high, inner_low = split_table(inner_table())
     twist_cos, twist_sin = twist_table()
@@ -159,13 +164,24 @@
     def whole(table):
         return pl.BlockSpec(table.shape, lambda pair: (0,) * table.ndim)
 
+    operands = [packed_rows] * 5 + [jnp.asarray(table) for table in tables]
+    in_specs = [frame_spec(t) for t in range(5)] + [whole(table) for table in tables]
+    kernel, aliases = channelize_kernel, {}
+    if into is not None:
+        aliases = {len(operands): 0}
+        operands.append(into)
+        in_specs.append(pl.BlockSpec(memory_space=pl.ANY))
+        kernel = channelize_more_kernel
     return pl.pallas_call(
-        channelize_kernel,
+        kernel,
         grid=(pairs,),
-        in_specs=[frame_spec(t) for t in range(5)] + [whole(table) for table in tables],
-        out_specs=pl.BlockSpec((GROUPS, 1, PAIR_ROWS, SECTION), lambda pair: (0, pair, 0, 0)),
-        out_shape=jax.ShapeDtypeStruct((GROUPS, pairs, PAIR_ROWS, SECTION), jnp.bfloat16),
+        in_specs=in_specs,
+        out_specs=pl.BlockSpec(
+            (GROUPS, 1, PAIR_ROWS, SECTION), lambda pair: (0, first_pair + pair, 0, 0)
+        ),
+        out_shape=jax.ShapeDtypeStruct((GROUPS, all_pairs, PAIR_ROWS, SECTION), jnp.bfloat16),
         scratch_shapes=[pltpu.VMEM((GROUPS * PAIR_ROWS, SECTION), jnp.float32)],
+        input_output_aliases=aliases,
         compiler_params=pltpu.CompilerParams(vmem_limit_bytes=VMEM_BYTES),
         cost_estimate=pl.CostEstimate(
             flops=pairs * 3 * 2 * 2 * 256 * 256 * 512,
@@ -173,7 +189,7 @@
             transcendentals=0,
         ),
         name="channelize",
-    )(*([packed_rows] * 5), *(jnp.asarray(table) for table in tables))
+    )(*operands)
 
 
 def spread_tables():
@@ -212,7 +228,7 @@
         out_shape=jax.ShapeDtypeStruct((2 * BEAMS, 2 * INPUTS), jnp.bfloat16),
         in_specs=[pl.BlockSpec(memory_space=pltpu.VMEM)] * 3,
         out_specs=pl.BlockSpec(memory_space=pltpu.VMEM),
-        compiler_params=pltpu.CompilerParams(vmem_limit_bytes=VMEM_BYTES),
+        compiler_params=pltpu.CompilerParams(vmem_limit_bytes=BEAM_VMEM_BYTES),
         cost_estimate=pl.CostEstimate(
             flops=2 * 2 * BEAMS * 512 * 512, bytes_accessed=5 * 2**20, transcendentals=0
         ),
@@ -234,24 +250,12 @@
     return real_part * real_part + imag_part * imag_part
 
 
-def start_kernel(weights_ref, spectra_ref, out):
+def beams_kernel(weights_ref, spectra_ref, out, total):
     powers = beam_block(weights_ref, spectra_ref)
 
     @pl.when(pl.program_id(0) == 0)
     def _():
-        out[...] = powers
-
-    @pl.when(pl.program_id(0) > 0)
-    def _():
-        out[...] += powers
-
-
-def finish_kernel(weights_ref, spectra_ref, before, out, total):
-    powers = beam_block(weights_ref, spectra_ref)
-
-    @pl.when(pl.program_id(0) == 0)
-    def _():
-        total[...] = before[...] + powers
+        total[...] = powers
 
     @pl.when(pl.program_id(0) > 0)
     def _():
@@ -268,43 +272,34 @@
         out[...] = jnp.where(lane < OUTER, sums[0], sums[1])
 
 
-def beam_call(weights, spectra, before=None):
+def beams(weights, spectra):
     pairs = spectra.shape[1]
-    in_specs = [
-        pl.BlockSpec((2 * BEAMS, 2 * INPUTS), lambda pair: (0, 0)),
-        pl.BlockSpec((GROUPS, 1, PAIR_ROWS, SECTION), lambda pair: (0, pair, 0, 0)),
-    ]
-    operands = [weights, spectra]
-    width = 2 * SECTION
-    scratch = []
-    if before is not None:
-        in_specs.append(pl.BlockSpec((BEAMS, width), lambda pair: (0, 0)))
-        operands.append(before)
-        scratch.append(pltpu.VMEM((BEAMS, width), jnp.float32))
-        width = SECTION
     return pl.pallas_call(
-        start_kernel if before is None else finish_kernel,
+        beams_kernel,
         grid=(pairs,),
-        in_specs=in_specs,
-        out_specs=pl.BlockSpec((BEAMS, width), lambda pair: (0, 0)),
-        out_shape=jax.ShapeDtypeStruct((BEAMS, width), jnp.float32),
-        scratch_shapes=scratch,
-        compiler_params=pltpu.CompilerParams(vmem_limit_bytes=VMEM_BYTES),
+        in_specs=[
+            pl.BlockSpec((2 * BEAMS, 2 * INPUTS), lambda pair: (0, 0)),
+            pl.BlockSpec((GROUPS, 1, PAIR_ROWS, SECTION), lambda pair: (0, pair, 0, 0)),
+        ],
+        out_specs=pl.BlockSpec((BEAMS, SECTION), lambda pair: (0, 0)),
+        out_shape=jax.ShapeDtypeStruct((BEAMS, SECTION), jnp.float32),
+        scratch_shapes=[pltpu.VMEM((BEAMS, 2 * SECTION), jnp.float32)],
+        compiler_params=pltpu.CompilerParams(vmem_limit_bytes=BEAM_VMEM_BYTES),
         cost_estimate=pl.CostEstimate(
             flops=pairs * 2 * 1536 * 512 * 256,
-            bytes_accessed=1536 * 512 * 2 + pairs * 262144 + 3 * 768 * 256 * 4,
+            bytes_accessed=1536 * 512 * 2 + pairs * 262144 + 768 * 128 * 4,
             transcendentals=0,
         ),
-        name="beams_start" if before is None else "beams_finish",
-    )(*operands)
-
-
-LATE_PAIRS = 4
+        name="beams",
+    )(weights, spectra)
+
+
+EARLY_PAIRS = 2
 
 
 def per_device(voltages, beam_weights):
     inputs_here, own_len = voltages.shape
-    spectra_here = own_len // CHANNELS
+    pairs = own_len // CHANNELS // 2
     rows = jnp.transpose(voltages.reshape(inputs_here, own_len // SECTION, SECTION), (1, 0, 2))
     rows = rows.reshape(own_len // SECTION * inputs_here, SECTION)
     rim = (TAPS - 1) * FRAME_ROWS
@@ -314,16 +309,16 @@
         "tm",
         [(i, i + 1) for i in range(devices - 1)],
     )
-    late = 2 * LATE_PAIRS
-    late_spectra = channelize(rows, spectra_here - late - 3, LATE_PAIRS)
-    late_turned = lax.all_to_all(late_spectra, "chan", 0, 0, tiled=True)
-    early = spectra_here - late
-    early_rows = jnp.concatenate([history + ZERO_SAMPLE, rows[: early * FRAME_ROWS]], axis=0)
-    early_spectra = channelize(early_rows, 0, early // 2)
-    early_turned = lax.all_to_all(early_spectra, "chan", 0, 0, tiled=True)
+    spectra = channelize(
+        rows, 2 * EARLY_PAIRS - 3, pairs - EARLY_PAIRS, EARLY_PAIRS, pairs
+    )
+    early_rows = jnp.concatenate(
+        [history + ZERO_SAMPLE, rows[: 2 * EARLY_PAIRS * FRAME_ROWS]], axis=0
+    )
+    spectra = channelize(early_rows, 0, EARLY_PAIRS, 0, pairs, spectra)
     weights = stacked_weights(beam_weights[0])
-    powers = beam_call(weights, late_turned)
-    averaged = beam_call(weights, early_turned, powers)
+    turned = lax.all_to_all(spectra, "chan", 0, 0, tiled=True)
+    averaged = beams(weights, turned)
     return lax.all_to_all(averaged[None], "chan", split_axis=1, concat_axis=2, tiled=True)
 
 

time: 147 us -> 140 us (0.952)
  the two profiles are of different devices: /device:TPU:9 before, /device:TPU:3 now
where the time goes in v2:
time: 140 us; the launch traced here: 139 us
  waiting for transfers between devices  61.7 us (44%)
  blocking collectives  28.3 us (20%)
  Pallas kernels  21.1 us (15%)
  starting transfers between devices  20.3 us (14%)
  local copies, waits for them, and re-layouts  5.45 us (4%)
  other arithmetic  2.1 us (2%)
    all_to_all x1, waiting for transfers between devices, per_device(): turned = lax.all_to_all(spectra, 'chan', 0, 0, tiled=True)  61.7 us
    all_to_all x1, blocking collectives, per_device(): lax.all_to_all(averaged[None], 'chan', split_axis=1, concat_axis=2, tiled...  28.3 us
    all_to_all x1, starting transfers between devices, per_device(): turned = lax.all_to_all(spectra, 'chan', 0, 0, tiled=True)  17.2 us
    pallas_call x2, Pallas kernels, channelize(): pl.pallas_call(kernel, grid=(pairs,), in_specs=in_specs, out_specs=pl.Blo...  14.3 us
    pallas_call x1, Pallas kernels, beams(): pl.pallas_call(beams_kernel, grid=(pairs,), in_specs=[pl.BlockSpec((2 * B...  5.79 us
    unnamed x10, local copies, waits for them, and re-layouts  3.59 us
    ppermute x1, starting transfers between devices, per_device(): lax.ppermute(rows[rows.shape[0] - rim:] - ZERO_SAMPLE, 'tm', [(i, i + 1)...  3.12 us
  transfers between devices with their start and end apart: 2, of which 1 were waited for; matrix products, arithmetic and copies ran while one was open for 1% of the time, Pallas kernels for 8%

profile of v2, /device:TPU:3, one launch (start us, length us, event | category | flops | bytes accessed | tf_op | source)
XLA Modules:
  0.0 139.1 jit_solution(15721160937989261665)
XLA Ops:
  0.0 1.1 slice_add_fusion
  1.1 3.1 %collective-permute-start = (s32[768,128]{1,0:T(8,128)S(1)}, s32[768,128]{1,0:T(8,128)S(1)}, u32[]{:S(2)}, u32[]{:S(2)}) collective-permute-start(s32[768,128]{1,0:T(8,128)S(1)} %bitcast.26), channel_id=1, source_target_pairs={{0,64},{64,128},{128,192},{192,256},{256,320},{320,384},{384,448},... | collective-permute-start | bytes 1179656 | tf_op jit(solution)/shard_map/ppermute | solution.py:307
  4.2 1.1 slice.14
  5.3 9.7 %channelize.2.refs_12_ = bf16[64,8,16,128]{3,2,1,0:T(8,128)(2,1)} custom-call(s32[4096,128]{1,0:T(8,128)} %bitcast.19, s32[4096,128]{1,0:T(8,128)} %bitcast.20, s32[4096,128]{1,0:T(8,128)} %bitcast.21, s32[4096,128]{1,0:T(8,128)} %bitcast.22, s32[4096,128]{1,0:T(8,128)} %bitcast.23, f32[4,64,128]{2,1,0:T(8,128)} %constant.22.clone.taper.refs_5_, ...), custom_call_target="tpu_custom_call" | custom-call | flops 2415919104 | bytes 5505024 | tf_op jit(solution)/shard_map/channelize/pallas_call | solution.py:175
  15.0 0.0 collective-permute-done
  15.0 1.0 pad_add_fusion.refs_0_.refs_1_.refs_2_.refs_3_.refs_4_
  16.0 4.6 %channelize.3 = bf16[64,8,16,128]{3,2,1,0:T(8,128)(2,1)} custom-call(s32[1792,128]{1,0:T(8,128)} %pad_add_fusion.refs_0_.refs_1_.refs_2_.refs_3_.refs_4_, s32[1792,128]{1,0:T(8,128)} %pad_add_fusion.refs_0_.refs_1_.refs_2_.refs_3_.refs_4_, s32[1792,128]{1,0:T(8,128)} %pad_add_fusion.refs_0_.refs_1_.refs_2_.refs_3_.refs_4_, ...), custom_call_target="tpu_custom_call", output_to_operand_aliasing={{}: (12, {})} | custom-call | flops 805306368 | bytes 1835008 | tf_op jit(solution)/shard_map/channelize/pallas_call | solution.py:175
  20.6 0.0 copy-start.2
  20.6 0.0 copy-start.3
  20.6 17.2 %all-to-all-start = ((bf16[64,8,16,128]{3,2,1,0:T(8,128)(2,1)}), bf16[64,8,16,128]{3,2,1,0:T(8,128)(2,1)S(1)}, u32[]{:S(2)}, u32[]{:S(2)}) async-start(bf16[64,8,16,128]{3,2,1,0:T(8,128)(2,1)} %channelize.3), calls=%async_computation | async-start | bytes 4194304 | tf_op jit(solution)/shard_map/all_to_all | solution.py:320
  37.9 0.0 copy-done.2
  37.9 0.0 copy-done.3
  37.9 0.0 copy-start.4
  37.9 1.0 copy-done.4
  38.9 1.0 stack_weights.1.weights_ref
  39.9 0.0 copy-start
  39.9 1.1 copy-done
  41.1 61.7 %all-to-all-done.spectra_ref = bf16[64,8,16,128]{3,2,1,0:T(8,128)(2,1)S(1)} async-done(((bf16[64,8,16,128]{3,2,1,0:T(8,128)(2,1)}), bf16[64,8,16,128]{3,2,1,0:T(8,128)(2,1)S(1)}, u32[]{:S(2)}, u32[]{:S(2)}) %all-to-all-start) | async-done | bytes 2097184 | tf_op jit(solution)/shard_map/all_to_all | solution.py:320
  102.8 0.0 copy-start.1
  102.8 1.4 %copy-done.1 = bf16[1536,512]{1,0:T(8,128)(2,1)S(1)} copy-done((bf16[1536,512]{1,0:T(8,128)(2,1)S(1)}, bf16[1536,512]{1,0:T(8,128)(2,1)}, u32[]{:S(2)}) %copy-start.1) | copy-done | bytes 1572888
  104.2 5.8 %beams.1 = f32[768,128]{1,0:T(8,128)S(1)} custom-call(bf16[1536,512]{1,0:T(8,128)(2,1)S(1)} %copy-done.1, bf16[64,8,16,128]{3,2,1,0:T(8,128)(2,1)S(1)} %all-to-all-done.spectra_ref), custom_call_target="tpu_custom_call" | custom-call | flops 3221225472 | bytes 4063232 | tf_op jit(solution)/shard_map/beams/pallas_call | solution.py:277
  110.0 28.3 %all_to_all.23 = f32[1,768,128]{2,0,1:T(1,128)S(1)} all-to-all(f32[1,768,128]{2,0,1:T(1,128)S(1)} %bitcast.16), channel_id=1, replica_groups=mesh['tm'=8,'chan'=64] {'chan'}, dimensions={1} | all-to-all | bytes 786432 | tf_op jit(solution)/shard_map/all_to_all | solution.py:322
  138.4 0.8 copy.27
  (1 shorter events, 0.0 us)
Async XLA Ops:
  1.1 13.9 %collective-permute-start = (s32[768,128]{1,0:T(8,128)S(1)}, s32[768,128]{1,0:T(8,128)S(1)}, u32[]{:S(2)}, u32[]{:S(2)}) collective-permute-start(s32[768,128]{1,0:T(8,128)S(1)} %bitcast.26), channel_id=1, source_target_pairs={{0,64},{64,128},{128,192},{192,256},{256,320},{320,384},{384,448},... | collective-permute-start | bytes 1179656 | tf_op jit(solution)/shard_map/ppermute | solution.py:307
  20.6 17.2 %copy-start.2 = (s32[1,768,256]{2,1,0:T(8,128)S(1)}, s32[1,768,256]{2,1,0:T(8,128)}, u32[]{:S(2)}) copy-start(s32[1,768,256]{2,1,0:T(8,128)} %param.19) | copy-start | bytes 2359300
  20.6 17.3 %copy-start.3 = (bf16[512,512]{1,0:T(8,128)(2,1)S(1)}, bf16[512,512]{1,0:T(8,128)(2,1)}, u32[]{:S(2)}) copy-start(bf16[512,512]{1,0:T(8,128)(2,1)} %constant.29.clone.upper) | copy-start | bytes 1572868
  20.6 82.2 %all-to-all-start = ((bf16[64,8,16,128]{3,2,1,0:T(8,128)(2,1)}), bf16[64,8,16,128]{3,2,1,0:T(8,128)(2,1)S(1)}, u32[]{:S(2)}, u32[]{:S(2)}) async-start(bf16[64,8,16,128]{3,2,1,0:T(8,128)(2,1)} %channelize.3), calls=%async_computation | async-start | bytes 4194304 | tf_op jit(solution)/shard_map/all_to_all | solution.py:320
  37.9 1.0 copy-start.4
  39.9 1.1 copy-start
  102.8 1.4 %copy-start.1 = (bf16[1536,512]{1,0:T(8,128)(2,1)S(1)}, bf16[1536,512]{1,0:T(8,128)(2,1)}, u32[]{:S(2)}) copy-start(bf16[1536,512]{1,0:T(8,128)(2,1)} %copy-done) | copy-start | bytes 4718596

commit v3 on v2

v3 whole, which is shorter than its diff:
```python
import functools
import math

import jax
import jax.numpy as jnp
import numpy as np
from jax import lax
from jax.experimental import pallas as pl
from jax.experimental.pallas import tpu as pltpu
from jax.sharding import PartitionSpec as P

INPUTS = 256
BEAMS = 768
CHANNELS = 8192
SECTION = 128
TAPS = 4
AVERAGE = 16
OUTER = 64
GROUPS = 64
ZERO_SAMPLE = 32 * 64 + 32
VMEM_BYTES = 60 * 1024 * 1024
EARLY_VMEM_BYTES = 51 * 1024 * 1024
BEAM_VMEM_BYTES = 51 * 1024 * 1024

INPUTS_HERE = 4
FRAME_ROWS = OUTER * INPUTS_HERE
PAIR_ROWS = 16
EARLY_PAIRS = 2


def split_table(table):
    high = table.astype(jnp.bfloat16)
    low = (table - np.asarray(high, np.float64)).astype(jnp.bfloat16)
    return np.asarray(high), np.asarray(low)


def pfb_taper():
    places = np.arange(TAPS * CHANNELS, dtype=np.float64)
    length = TAPS * CHANNELS
    offsets = (places - 0.5 * length + 0.5) / CHANNELS
    hann_window = 0.5 - 0.5 * np.cos(2.0 * math.pi * (places + 0.5) / length)
    taper = np.sinc(offsets) * hann_window
    return taper.astype(np.float32).reshape(TAPS, OUTER, SECTION)


def phasors(left_index, right_index, length):
    turns = np.outer(left_index, right_index) % length
    angles = turns * (-2.0 * math.pi / length)
    return np.cos(angles), np.sin(angles)


def outer_table():
    cos_part, sin_part = phasors(np.arange(OUTER), np.arange(OUTER), OUTER)
    table = np.zeros((2, 2, OUTER, 2, 2, OUTER))
    for f in range(2):
        table[0, f, :, f, 0, :] = cos_part
        table[0, f, :, f, 1, :] = -sin_part
        table[1, f, :, f, 0, :] = sin_part
        table[1, f, :, f, 1, :] = cos_part
    return table.reshape(4 * OUTER, 4 * OUTER)


def twist_table():
    norm = 1.0 / (32.0 * math.sqrt(CHANNELS))
    cos_part, sin_part = phasors(np.arange(OUTER), np.arange(SECTION), CHANNELS)
    return (
        np.tile(cos_part * norm, (2, 1)).astype(np.float32),
        np.tile(sin_part * norm, (2, 1)).astype(np.float32),
    )


def inner_table():
    channel = np.arange(SECTION).reshape(GROUPS, 2).T
    table = np.zeros((2, 2, GROUPS, 2, SECTION))
    for half in range(2):
        cos_part, sin_part = phasors(channel[half], np.arange(SECTION), SECTION)
        table[half, 0, :, 0, :] = cos_part
        table[half, 0, :, 1, :] = -sin_part
        table[half, 1, :, 0, :] = sin_part
        table[half, 1, :, 1, :] = cos_part
    return table.reshape(4 * GROUPS, 2 * SECTION)


def two_halves(values):
    high = values.astype(jnp.bfloat16)
    low = (values - high.astype(jnp.float32)).astype(jnp.bfloat16)
    return high, low


def careful_dot(left_high, left_low, right, contract):
    right_high, right_low = two_halves(right)
    dims = (contract, ((), ()))

    def dot(left, values):
        return lax.dot_general(left, values, dims, preferred_element_type=jnp.float32)

    return dot(left_high, right_high) + (dot(left_high, right_low) + dot(left_low, right_high))


def channelize_pair(load, tables, waves, strided):
    columns = []
    for i in range(INPUTS_HERE):
        summed = {}
        for t in range(TAPS + 1):
            packed = load(t, i)
            parts = (
                ((packed >> 6) - 32).astype(jnp.float32),
                ((packed & 63) - 32).astype(jnp.float32),
            )
            for f in range(2):
                if 0 <= t - f < TAPS:
                    tap = waves[(t - f) * OUTER : (t - f + 1) * OUTER]
                    for part in range(2):
                        term = parts[part] * tap
                        key = (f, part)
                        summed[key] = summed[key] + term if key in summed else term
        columns.append(
            jnp.concatenate([summed[f, part] for f in range(2) for part in range(2)], axis=0)
        )
    frames = jnp.concatenate(columns, axis=1)
    size = 4 * OUTER
    first = careful_dot(tables[:size], tables[size : 2 * size], frames, ((1,), (0,)))
    cos_part = waves[TAPS * OUTER : TAPS * OUTER + SECTION]
    sin_part = waves[TAPS * OUTER + SECTION : TAPS * OUTER + 2 * SECTION]
    turned = []
    for i in range(INPUTS_HERE):
        real_part = first[:SECTION, i * SECTION : (i + 1) * SECTION]
        imag_part = first[SECTION:, i * SECTION : (i + 1) * SECTION]
        turned.append(
            jnp.concatenate(
                [
                    real_part * cos_part - imag_part * sin_part,
                    real_part * sin_part + imag_part * cos_part,
                ],
                axis=1,
            )
        )
    turned = jnp.concatenate(turned, axis=0)
    spectra = careful_dot(
        tables[2 * size : 3 * size], tables[3 * size : 4 * size], turned, ((1,), (1,))
    )
    for half in range(2):
        for part in range(2):
            top = (half * 2 + part) * GROUPS
            for i in range(INPUTS_HERE):
                row = half * 8 + i * 2 + part
                strided[pl.ds(row, GROUPS, stride=PAIR_ROWS), :] = spectra[
                    top : top + GROUPS, i * SECTION : (i + 1) * SECTION
                ]
    return strided[...].astype(jnp.bfloat16).reshape(GROUPS, PAIR_ROWS, SECTION)


def late_kernel(
    rows, tables_in, waves_in, out,
    frames, tables, waves, strided, staged, frame_sem, table_sem, out_sem,
):
    pairs = staged.shape[0]
    start = (2 * EARLY_PAIRS - (TAPS - 1)) * FRAME_ROWS
    step = 2 * FRAME_ROWS
    lead = (TAPS - 1) * FRAME_ROWS

    def fetch(pair):
        at = 0 if isinstance(pair, int) else lead + pair * step
        size = lead + step if isinstance(pair, int) else step
        return pltpu.make_async_copy(
            rows.at[pl.ds(start + at, size)], frames.at[pl.ds(at, size)], frame_sem.at[pair]
        )

    def send(pair):
        return pltpu.make_async_copy(
            staged.at[pair], out.at[:, EARLY_PAIRS + pair], out_sem.at[pair]
        )

    table_copies = [
        pltpu.make_async_copy(waves_in, waves, table_sem.at[0]),
        pltpu.make_async_copy(tables_in, tables, table_sem.at[1]),
    ]
    table_copies[0].start()
    fetch(0).start()
    table_copies[1].start()

    @pl.loop(1, pairs)
    def _(pair):
        fetch(pair).start()

    for copy in table_copies:
        copy.wait()
    fetch(0).wait()

    @pl.loop(0, pairs)
    def _(pair):
        @pl.when(pair > 0)
        def _():
            fetch(pair).wait()

        def load(t, i):
            return frames[
                pl.ds(pair * step + t * FRAME_ROWS + i, OUTER, stride=INPUTS_HERE), :
            ]

        staged[pair] = channelize_pair(load, tables, waves, strided)
        send(pair).start()

    @pl.loop(0, pairs)
    def _(pair):
        send(pair).wait()


def channelizer_tables():
    outer_high, outer_low = split_table(outer_table())
    inner_high, inner_low = split_table(inner_table())
    twist_cos, twist_sin = twist_table()
    tables = np.concatenate([outer_high, outer_low, inner_high, inner_low], axis=0)
    taper = pfb_taper().reshape(TAPS * OUTER, SECTION)
    waves = np.concatenate([taper, twist_cos, twist_sin], axis=0)
    return jnp.asarray(tables), jnp.asarray(waves)


def channelizer_cost(pairs):
    return pl.CostEstimate(
        flops=pairs * 3 * 2 * 2 * 256 * 256 * 512,
        bytes_accessed=pairs * 2 * 262144 + 2**20,
        transcendentals=0,
    )


def channelize_late(rows, tables, waves, all_pairs):
    pairs = all_pairs - EARLY_PAIRS
    return pl.pallas_call(
        late_kernel,
        in_specs=[pl.BlockSpec(memory_space=pl.ANY)] * 3,
        out_specs=pl.BlockSpec(memory_space=pl.ANY),
        out_shape=jax.ShapeDtypeStruct((GROUPS, all_pairs, PAIR_ROWS, SECTION), jnp.bfloat16),
        scratch_shapes=[
            pltpu.VMEM(((2 * pairs + TAPS - 1) * FRAME_ROWS, SECTION), jnp.int32),
            pltpu.VMEM(tables.shape, tables.dtype),
            pltpu.VMEM(waves.shape, waves.dtype),
            pltpu.VMEM((GROUPS * PAIR_ROWS, SECTION), jnp.float32),
            pltpu.VMEM((pairs, GROUPS, PAIR_ROWS, SECTION), jnp.bfloat16),
            pltpu.SemaphoreType.DMA((pairs,)),
            pltpu.SemaphoreType.DMA((2,)),
            pltpu.SemaphoreType.DMA((pairs,)),
        ],
        compiler_params=pltpu.CompilerParams(vmem_limit_bytes=VMEM_BYTES),
        cost_estimate=channelizer_cost(pairs),
        name="channelize_late",
    )(rows, tables, waves)


def early_kernel(
    history, rows_in, tables, waves, into, out, rows, strided, staged, row_sem, out_sem
):
    rim = TAPS - 1
    fetch = pltpu.make_async_copy(rows_in.at[pl.ds(0, rows.shape[0])], rows, row_sem)
    fetch.start()
    fetch.wait()
    copies = []
    for pair in range(EARLY_PAIRS):

        def load(t, i, pair=pair):
            frame = 2 * pair + t - rim
            if frame < 0:
                at = (frame + rim) * FRAME_ROWS + i
                return history[pl.ds(at, OUTER, stride=INPUTS_HERE), :] + ZERO_SAMPLE
            return rows[pl.ds(frame * FRAME_ROWS + i, OUTER, stride=INPUTS_HERE), :]

        staged[pair] = channelize_pair(load, tables, waves, strided)
        copies.append(pltpu.make_async_copy(staged.at[pair], out.at[:, pair], out_sem.at[pair]))
        copies[-1].start()
    for copy in copies:
        copy.wait()


def channelize_early(history, rows, tables, waves, into):
    near, far = pl.BlockSpec(memory_space=pltpu.VMEM), pl.BlockSpec(memory_space=pl.ANY)
    return pl.pallas_call(
        early_kernel,
        in_specs=[near, far, near, near, far],
        out_specs=far,
        out_shape=jax.ShapeDtypeStruct(into.shape, into.dtype),
        scratch_shapes=[
            pltpu.VMEM((2 * EARLY_PAIRS * FRAME_ROWS, SECTION), jnp.int32),
            pltpu.VMEM((GROUPS * PAIR_ROWS, SECTION), jnp.float32),
            pltpu.VMEM((EARLY_PAIRS, GROUPS, PAIR_ROWS, SECTION), jnp.bfloat16),
            pltpu.SemaphoreType.DMA,
            pltpu.SemaphoreType.DMA((EARLY_PAIRS,)),
        ],
        input_output_aliases={4: 0},
        compiler_params=pltpu.CompilerParams(vmem_limit_bytes=EARLY_VMEM_BYTES),
        cost_estimate=channelizer_cost(EARLY_PAIRS),
        name="channelize_early",
    )(history, rows, tables, waves, into)


def spread_tables():
    even = np.zeros((INPUTS, INPUTS, 2))
    odd = np.zeros((INPUTS, INPUTS, 2))
    even[np.arange(INPUTS), np.arange(INPUTS), 0] = 1.0
    odd[np.arange(INPUTS), np.arange(INPUTS), 1] = 1.0
    even = even.reshape(INPUTS, 2 * INPUTS)
    odd = odd.reshape(INPUTS, 2 * INPUTS)
    upper = np.concatenate([even, -odd], axis=0)
    lower = np.concatenate([odd, even], axis=0)
    return upper.astype(jnp.bfloat16), lower.astype(jnp.bfloat16)


def weights_kernel(packed_ref, upper, lower, out):
    packed = packed_ref[...]
    parts = jnp.concatenate(
        [
            ((packed >> 6) - 32).astype(jnp.float32).astype(jnp.bfloat16),
            ((packed & 63) - 32).astype(jnp.float32).astype(jnp.bfloat16),
        ],
        axis=1,
    )
    out[:BEAMS] = jnp.dot(parts, upper[...], preferred_element_type=jnp.float32).astype(
        jnp.bfloat16
    )
    out[BEAMS:] = jnp.dot(parts, lower[...], preferred_element_type=jnp.float32).astype(
        jnp.bfloat16
    )


def stacked_weights(packed):
    upper, lower = spread_tables()
    tables = (packed, jnp.asarray(upper), jnp.asarray(lower))
    return pl.pallas_call(
        weights_kernel,
        grid=(1,),
        out_shape=jax.ShapeDtypeStruct((2 * BEAMS, 4 * INPUTS), jnp.bfloat16),
        in_specs=[pl.BlockSpec(table.shape, lambda _: (0, 0)) for table in tables],
        out_specs=pl.BlockSpec((2 * BEAMS, 2 * INPUTS), lambda _: (0, 0)),
        compiler_params=pltpu.CompilerParams(vmem_limit_bytes=EARLY_VMEM_BYTES),
        cost_estimate=pl.CostEstimate(
            flops=2 * 2 * BEAMS * 512 * 512, bytes_accessed=5 * 2**20, transcendentals=0
        ),
        name="stack_weights",
    )(*tables)


BEAM_BLOCK = 256


def beams_kernel(weights_in, spectra_ref, out, weights_ref, total, weight_sem):
    pairs = range(spectra_ref.shape[1])
    blocks = range(0, BEAMS, BEAM_BLOCK)

    def fetch_weights(block, part):
        rows = pl.ds(part * BEAMS + block * BEAM_BLOCK, BEAM_BLOCK)
        return pltpu.make_async_copy(
            weights_in.at[rows, pl.ds(0, 2 * INPUTS)], weights_ref.at[rows], weight_sem.at[block, part]
        )

    for block in range(len(blocks)):
        for part in range(2):
            fetch_weights(block, part).start()

    def paired(pair):
        spectra = spectra_ref[:, pair].astype(jnp.float32)
        return jnp.concatenate(
            [
                spectra[:, half * 8 : half * 8 + 8].reshape(2 * INPUTS, SECTION).astype(jnp.bfloat16)
                for half in range(2)
            ],
            axis=1,
        )

    def formed(at, values):
        return jnp.dot(
            weights_ref[at : at + BEAM_BLOCK], values, preferred_element_type=jnp.float32
        )

    values = {}
    for block, at in enumerate(blocks):
        for part in range(2):
            fetch_weights(block, part).wait()
        for pair in pairs:
            if block == 0:
                values[pair] = paired(pair)
            real_part = formed(at, values[pair])
            imag_part = formed(BEAMS + at, values[pair])
            powers = real_part * real_part + imag_part * imag_part
            total[at : at + BEAM_BLOCK] = (
                powers if pair == 0 else total[at : at + BEAM_BLOCK] + powers
            )
    scale = 1.0 / (24.0 * math.sqrt(INPUTS)) ** 2 / AVERAGE
    lane = lax.broadcasted_iota(jnp.int32, (BEAMS, SECTION), 1)
    sums = []
    for half in range(2):
        part = total[:, half * SECTION : (half + 1) * SECTION]
        sums.append((part + pltpu.roll(part, OUTER, 1)) * scale)
    out[...] = jnp.where(lane < OUTER, sums[0], sums[1])


def beams(weights, spectra):
    pairs = spectra.shape[1]
    return pl.pallas_call(
        beams_kernel,
        in_specs=[pl.BlockSpec(memory_space=pl.ANY), pl.BlockSpec(memory_space=pltpu.VMEM)],
        out_specs=pl.BlockSpec(memory_space=pltpu.VMEM),
        out_shape=jax.ShapeDtypeStruct((BEAMS, SECTION), jnp.float32),
        scratch_shapes=[
            pltpu.VMEM((2 * BEAMS, 2 * INPUTS), weights.dtype),
            pltpu.VMEM((BEAMS, 2 * SECTION), jnp.float32),
            pltpu.SemaphoreType.DMA((BEAMS // BEAM_BLOCK, 2)),
        ],
        compiler_params=pltpu.CompilerParams(vmem_limit_bytes=BEAM_VMEM_BYTES),
        cost_estimate=pl.CostEstimate(
            flops=pairs * 2 * 1536 * 512 * 256,
            bytes_accessed=1536 * 512 * 2 + pairs * 262144 + 768 * 128 * 4,
            transcendentals=0,
        ),
        name="beams",
    )(weights, spectra)


def per_device(voltages, beam_weights):
    inputs_here, own_len = voltages.shape
    pairs = own_len // CHANNELS // 2
    rows = jnp.transpose(voltages.reshape(inputs_here, own_len // SECTION, SECTION), (1, 0, 2))
    rows = rows.reshape(own_len // SECTION * inputs_here, SECTION)
    rim = (TAPS - 1) * FRAME_ROWS
    devices = lax.axis_size("tm")
    history = lax.ppermute(
        rows[rows.shape[0] - rim :] - ZERO_SAMPLE,
        "tm",
        [(i, i + 1) for i in range(devices - 1)],
    )
    tables, waves = channelizer_tables()
    spectra = channelize_late(rows, tables, waves, pairs)
    spectra = channelize_early(history, rows, tables, waves, spectra)
    weights = stacked_weights(beam_weights[0])
    turned = lax.all_to_all(spectra, "chan", 0, 0, tiled=True)
    averaged = beams(weights, turned)
    return lax.all_to_all(averaged[None], "chan", split_axis=1, concat_axis=2, tiled=True)


def solution(mesh):
    return jax.shard_map(
        per_device,
        mesh=mesh,
        in_specs=(P("chan", "tm"), P("chan", None, None)),
        out_specs=P("tm", "chan", None),
        check_vma=False,
    )
```

time: 140 us -> 134 us (0.957)
  local copies, waits for them, and re-layouts: 5.45 us -> 1.85 us
    unnamed x10, local copies, waits for them, and re-layouts: 3.59 us -> 1.06 us
  transfers between devices with their start and end apart: 2 -> 2, of which waited for: 1 -> 1; matrix products, arithmetic and copies ran while one was open for 1% -> 0% of each run, Pallas kernels for 8% -> 9%
where the time goes in v3:
time: 134 us
  waiting for transfers between devices  61.8 us (46%)
  blocking collectives  28.2 us (21%)
  starting transfers between devices  20.3 us (15%)
  Pallas kernels  20.3 us (15%)
  local copies, waits for them, and re-layouts  1.85 us (1%)
    all_to_all x1, waiting for transfers between devices, per_device(): turned = lax.all_to_all(spectra, 'chan', 0, 0, tiled=True)  61.8 us
    all_to_all x1, blocking collectives, per_device(): lax.all_to_all(averaged[None], 'chan', split_axis=1, concat_axis=2, tiled...  28.2 us
    all_to_all x1, starting transfers between devices, per_device(): turned = lax.all_to_all(spectra, 'chan', 0, 0, tiled=True)  17.2 us
    pallas_call x1, Pallas kernels, channelize_late(): pl.pallas_call(late_kernel, in_specs=[pl.BlockSpec(memory_space=pl.ANY)]...  9.34 us
    pallas_call x1, Pallas kernels, beams(): pl.pallas_call(beams_kernel, in_specs=[pl.BlockSpec(memory_space=pl.ANY),...  4.94 us
    pallas_call x1, Pallas kernels, channelize_early(): pl.pallas_call(early_kernel, in_specs=[near, far, near, near, far], out_s...  3.81 us
    ppermute x1, starting transfers between devices, per_device(): lax.ppermute(rows[rows.shape[0] - rim:] - ZERO_SAMPLE, 'tm', [(i, i + 1)...  3.12 us
  transfers between devices with their start and end apart: 2, of which 1 were waited for; matrix products, arithmetic and copies ran while one was open for 0% of the time, Pallas kernels for 9%

profile of v3, /device:TPU:3, one launch (start us, length us, event | category | flops | bytes accessed | tf_op | source)
XLA Modules:
  0.0 133.7 jit_solution(11483570714094843577)
XLA Ops:
  0.0 1.1 slice_add_fusion
  1.1 3.1 %collective-permute-start = (s32[768,128]{1,0:T(8,128)S(1)}, s32[768,128]{1,0:T(8,128)S(1)}, u32[]{:S(2)}, u32[]{:S(2)}) collective-permute-start(s32[768,128]{1,0:T(8,128)S(1)} %bitcast.20), channel_id=1, source_target_pairs={{0,64},{64,128},{128,192},{192,256},{256,320},{320,384},{384,448},... | collective-permute-start | bytes 1179656 | tf_op jit(solution)/shard_map/ppermute | solution.py:424
  4.2 0.0 copy-start.1
  4.2 0.0 copy-start.4
  4.2 9.3 %channelize_late.1.into = bf16[64,8,16,128]{3,2,1,0:T(8,128)(2,1)} custom-call(s32[4096,128]{1,0:T(8,128)} %bitcast.17, bf16[1024,256]{1,0:T(8,128)(2,1)} %constant.11.clone.tables_in.tables, f32[512,128]{1,0:T(8,128)} %constant.12.clone.waves_in.waves), custom_call_target="tpu_custom_call" | custom-call | flops 2415919104 | bytes 4194304 | tf_op jit(solution)/shard_map/channelize_late/pallas_call | solution.py:229
  13.6 0.0 collective-permute-done.history
  13.6 0.0 copy-done.1
  13.6 0.0 copy-done.4
  13.6 3.8 %channelize_early.1 = bf16[64,8,16,128]{3,2,1,0:T(8,128)(2,1)} custom-call(s32[768,128]{1,0:T(8,128)S(1)} %collective-permute-done.history, s32[4096,128]{1,0:T(8,128)} %bitcast.18, bf16[1024,256]{1,0:T(8,128)(2,1)S(1)} %copy-done.1, f32[512,128]{1,0:T(8,128)S(1)} %copy-done.4, ...), custom_call_target="tpu_custom_call", output_to_operand_aliasing={{}: (4, {})} | custom-call | flops 805306368 | bytes 2097152 | tf_op jit(solution)/shard_map/channelize_early/pallas_call | solution.py:276
  17.4 0.0 copy-start
  17.4 0.0 copy-start.2
  17.4 17.2 %all-to-all-start = ((bf16[64,8,16,128]{3,2,1,0:T(8,128)(2,1)}), bf16[64,8,16,128]{3,2,1,0:T(8,128)(2,1)S(1)}, u32[]{:S(2)}, u32[]{:S(2)}) async-start(bf16[64,8,16,128]{3,2,1,0:T(8,128)(2,1)} %channelize_early.1), calls=%async_computation | async-start | bytes 4194304 | tf_op jit(solution)/shard_map/all_to_all | solution.py:433
  34.7 0.0 copy-done
  34.7 0.0 copy-done.2
  34.7 0.0 copy-start.3
  34.7 1.0 copy-done.3
  35.8 2.2 %stack_weights.1.weights_in = bf16[1536,1024]{1,0:T(8,128)(2,1)} custom-call(s32[768,256]{1,0:T(8,128)S(1)} %bitcast.14, bf16[512,512]{1,0:T(8,128)(2,1)S(1)} %copy-done.3, bf16[512,512]{1,0:T(8,128)(2,1)S(1)} %copy-done.2), custom_call_target="tpu_custom_call" | custom-call | flops 805306368 | bytes 5242880 | tf_op jit(solution)/shard_map/stack_weights/pallas_call | solution.py:327
  38.0 61.8 %all-to-all-done.spectra_ref = bf16[64,8,16,128]{3,2,1,0:T(8,128)(2,1)S(1)} async-done(((bf16[64,8,16,128]{3,2,1,0:T(8,128)(2,1)}), bf16[64,8,16,128]{3,2,1,0:T(8,128)(2,1)S(1)}, u32[]{:S(2)}, u32[]{:S(2)}) %all-to-all-start) | async-done | bytes 2097184 | tf_op jit(solution)/shard_map/all_to_all | solution.py:433
  99.8 4.9 %beams.1 = f32[768,128]{1,0:T(8,128)S(1)} custom-call(bf16[1536,1024]{1,0:T(8,128)(2,1)} %stack_weights.1.weights_in, bf16[64,8,16,128]{3,2,1,0:T(8,128)(2,1)S(1)} %all-to-all-done.spectra_ref), custom_call_target="tpu_custom_call" | custom-call | flops 3221225472 | bytes 4063232 | tf_op jit(solution)/shard_map/beams/pallas_call | solution.py:397
  104.7 28.2 %all_to_all.23 = f32[1,768,128]{2,0,1:T(1,128)S(1)} all-to-all(f32[1,768,128]{2,0,1:T(1,128)S(1)} %bitcast.15), channel_id=1, replica_groups=mesh['tm'=8,'chan'=64] {'chan'}, dimensions={1} | all-to-all | bytes 786432 | tf_op jit(solution)/shard_map/all_to_all | solution.py:435
  132.9 0.8 copy.15
Async XLA Ops:
  1.1 12.5 %collective-permute-start = (s32[768,128]{1,0:T(8,128)S(1)}, s32[768,128]{1,0:T(8,128)S(1)}, u32[]{:S(2)}, u32[]{:S(2)}) collective-permute-start(s32[768,128]{1,0:T(8,128)S(1)} %bitcast.20), channel_id=1, source_target_pairs={{0,64},{64,128},{128,192},{192,256},{256,320},{320,384},{384,448},... | collective-permute-start | bytes 1179656 | tf_op jit(solution)/shard_map/ppermute | solution.py:424
  4.2 9.4 %copy-start.1 = (bf16[1024,256]{1,0:T(8,128)(2,1)S(1)}, bf16[1024,256]{1,0:T(8,128)(2,1)}, u32[]{:S(2)}) copy-start(bf16[1024,256]{1,0:T(8,128)(2,1)} %constant.11.clone.tables_in.tables) | copy-start | bytes 1572868
  4.2 9.4 %copy-start.4 = (f32[512,128]{1,0:T(8,128)S(1)}, f32[512,128]{1,0:T(8,128)}, u32[]{:S(2)}) copy-start(f32[512,128]{1,0:T(8,128)} %constant.12.clone.waves_in.waves) | copy-start | bytes 786436
  17.4 17.3 %copy-start = (s32[1,768,256]{2,1,0:T(8,128)S(1)}, s32[1,768,256]{2,1,0:T(8,128)}, u32[]{:S(2)}) copy-start(s32[1,768,256]{2,1,0:T(8,128)} %param.7) | copy-start | bytes 2359300
  17.4 17.3 %copy-start.2 = (bf16[512,512]{1,0:T(8,128)(2,1)S(1)}, bf16[512,512]{1,0:T(8,128)(2,1)}, u32[]{:S(2)}) copy-start(bf16[512,512]{1,0:T(8,128)(2,1)} %constant.14.clone.lower) | copy-start | bytes 1572868
  17.4 82.3 %all-to-all-start = ((bf16[64,8,16,128]{3,2,1,0:T(8,128)(2,1)}), bf16[64,8,16,128]{3,2,1,0:T(8,128)(2,1)S(1)}, u32[]{:S(2)}, u32[]{:S(2)}) async-start(bf16[64,8,16,128]{3,2,1,0:T(8,128)(2,1)} %channelize_early.1), calls=%async_computation | async-start | bytes 4194304 | tf_op jit(solution)/shard_map/all_to_all | solution.py:433
  34.7 1.0 copy-start.3

commit v4 on v3

--- a/solution.py
+++ b/solution.py
@@ -18,9 +18,10 @@
 OUTER = 64
 GROUPS = 64
 ZERO_SAMPLE = 32 * 64 + 32
-VMEM_BYTES = 60 * 1024 * 1024
-EARLY_VMEM_BYTES = 51 * 1024 * 1024
-BEAM_VMEM_BYTES = 51 * 1024 * 1024
+TABLE_ROOM = 6144
+LATE_VMEM_BYTES = 51 * 1024 * 1024
+EARLY_VMEM_BYTES = 50 * 1024 * 1024
+BEAM_VMEM_BYTES = 32 * 1024 * 1024
 
 INPUTS_HERE = 4
 FRAME_ROWS = OUTER * INPUTS_HERE
@@ -172,8 +173,8 @@
         )
 
     table_copies = [
-        pltpu.make_async_copy(waves_in, waves, table_sem.at[0]),
-        pltpu.make_async_copy(tables_in, tables, table_sem.at[1]),
+        pltpu.make_async_copy(waves_in.at[pl.ds(0, waves.shape[0])], waves, table_sem.at[0]),
+        pltpu.make_async_copy(tables_in.at[pl.ds(0, tables.shape[0])], tables, table_sem.at[1]),
     ]
     table_copies[0].start()
     fetch(0).start()
@@ -213,7 +214,7 @@
     tables = np.concatenate([outer_high, outer_low, inner_high, inner_low], axis=0)
     taper = pfb_taper().reshape(TAPS * OUTER, SECTION)
     waves = np.concatenate([taper, twist_cos, twist_sin], axis=0)
-    return jnp.asarray(tables), jnp.asarray(waves)
+    return tables, waves
 
 
 def channelizer_cost(pairs):
@@ -226,6 +227,10 @@
 
 def channelize_late(rows, tables, waves, all_pairs):
     pairs = all_pairs - EARLY_PAIRS
+    padded = [
+        jnp.asarray(np.pad(table, ((0, TABLE_ROOM - table.shape[0]), (0, 0))))
+        for table in (tables, waves)
+    ]
     return pl.pallas_call(
         late_kernel,
         in_specs=[pl.BlockSpec(memory_space=pl.ANY)] * 3,
@@ -241,10 +246,10 @@
             pltpu.SemaphoreType.DMA((2,)),
             pltpu.SemaphoreType.DMA((pairs,)),
         ],
-        compiler_params=pltpu.CompilerParams(vmem_limit_bytes=VMEM_BYTES),
+        compiler_params=pltpu.CompilerParams(vmem_limit_bytes=LATE_VMEM_BYTES),
         cost_estimate=channelizer_cost(pairs),
         name="channelize_late",
-    )(rows, tables, waves)
+    )(rows, *padded)
 
 
 def early_kernel(
@@ -289,7 +294,7 @@
         compiler_params=pltpu.CompilerParams(vmem_limit_bytes=EARLY_VMEM_BYTES),
         cost_estimate=channelizer_cost(EARLY_PAIRS),
         name="channelize_early",
-    )(history, rows, tables, waves, into)
+    )(history, rows, jnp.asarray(tables), jnp.asarray(waves), into)
 
 
 def spread_tables():
@@ -323,37 +328,25 @@
 
 def stacked_weights(packed):
     upper, lower = spread_tables()
-    tables = (packed, jnp.asarray(upper), jnp.asarray(lower))
     return pl.pallas_call(
         weights_kernel,
-        grid=(1,),
-        out_shape=jax.ShapeDtypeStruct((2 * BEAMS, 4 * INPUTS), jnp.bfloat16),
-        in_specs=[pl.BlockSpec(table.shape, lambda _: (0, 0)) for table in tables],
-        out_specs=pl.BlockSpec((2 * BEAMS, 2 * INPUTS), lambda _: (0, 0)),
-        compiler_params=pltpu.CompilerParams(vmem_limit_bytes=EARLY_VMEM_BYTES),
+        out_shape=jax.ShapeDtypeStruct((2 * BEAMS, 2 * INPUTS), jnp.bfloat16),
+        in_specs=[pl.BlockSpec(memory_space=pltpu.VMEM)] * 3,
+        out_specs=pl.BlockSpec(memory_space=pltpu.VMEM),
+        compiler_params=pltpu.CompilerParams(vmem_limit_bytes=BEAM_VMEM_BYTES),
         cost_estimate=pl.CostEstimate(
             flops=2 * 2 * BEAMS * 512 * 512, bytes_accessed=5 * 2**20, transcendentals=0
         ),
         name="stack_weights",
-    )(*tables)
+    )(packed, jnp.asarray(upper), jnp.asarray(lower))
 
 
 BEAM_BLOCK = 256
 
 
-def beams_kernel(weights_in, spectra_ref, out, weights_ref, total, weight_sem):
+def beams_kernel(weights_ref, spectra_ref, out, total):
     pairs = range(spectra_ref.shape[1])
     blocks = range(0, BEAMS, BEAM_BLOCK)
-
-    def fetch_weights(block, part):
-        rows = pl.ds(part * BEAMS + block * BEAM_BLOCK, BEAM_BLOCK)
-        return pltpu.make_async_copy(
-            weights_in.at[rows, pl.ds(0, 2 * INPUTS)], weights_ref.at[rows], weight_sem.at[block, part]
-        )
-
-    for block in range(len(blocks)):
-        for part in range(2):
-            fetch_weights(block, part).start()
 
     def paired(pair):
         spectra = spectra_ref[:, pair].astype(jnp.float32)
@@ -372,8 +365,6 @@
 
     values = {}
     for block, at in enumerate(blocks):
-        for part in range(2):
-            fetch_weights(block, part).wait()
         for pair in pairs:
             if block == 0:
                 values[pair] = paired(pair)
@@ -396,14 +387,10 @@
     pairs = spectra.shape[1]
     return pl.pallas_call(
         beams_kernel,
-        in_specs=[pl.BlockSpec(memory_space=pl.ANY), pl.BlockSpec(memory_space=pltpu.VMEM)],
+        in_specs=[pl.BlockSpec(memory_space=pltpu.VMEM)] * 2,
         out_specs=pl.BlockSpec(memory_space=pltpu.VMEM),
         out_shape=jax.ShapeDtypeStruct((BEAMS, SECTION), jnp.float32),
-        scratch_shapes=[
-            pltpu.VMEM((2 * BEAMS, 2 * INPUTS), weights.dtype),
-            pltpu.VMEM((BEAMS, 2 * SECTION), jnp.float32),
-            pltpu.SemaphoreType.DMA((BEAMS // BEAM_BLOCK, 2)),
-        ],
+        scratch_shapes=[pltpu.VMEM((BEAMS, 2 * SECTION), jnp.float32)],
         compiler_params=pltpu.CompilerParams(vmem_limit_bytes=BEAM_VMEM_BYTES),
         cost_estimate=pl.CostEstimate(
             flops=pairs * 2 * 1536 * 512 * 256,
@@ -428,8 +415,10 @@
     )
     tables, waves = channelizer_tables()
     spectra = channelize_late(rows, tables, waves, pairs)
+    spectra, packed_weights = lax.optimization_barrier((spectra, beam_weights[0]))
+    weights = stacked_weights(packed_weights)
     spectra = channelize_early(history, rows, tables, waves, spectra)
-    weights = stacked_weights(beam_weights[0])
+    spectra, weights = lax.optimization_barrier((spectra, weights))
     turned = lax.all_to_all(spectra, "chan", 0, 0, tiled=True)
     averaged = beams(weights, turned)
     return lax.all_to_all(averaged[None], "chan", split_axis=1, concat_axis=2, tiled=True)

time: 134 us -> 132 us (0.985)
  blocking collectives: 28.2 us -> 110 us
  waiting for transfers between devices: 61.8 us -> 0.01 us
  starting transfers between devices: 20.3 us -> 3.12 us
  Pallas kernels: 20.3 us -> 16.6 us
    all_to_all x0 -> x1, blocking collectives: none -> 82 us  [per_device(): turned = lax.all_to_all(spectra, 'chan', 0, 0, tiled=True)]
    all_to_all x1 -> x0, waiting for transfers between devices: 61.8 us -> none  [per_device(): turned = lax.all_to_all(spectra, 'chan', 0, 0, tiled=True)]
    all_to_all x1 -> x0, starting transfers between devices: 17.2 us -> none  [per_device(): turned = lax.all_to_all(spectra, 'chan', 0, 0, tiled=True)]
    pallas_call x2, Pallas kernels: 7.16 us -> 4.49 us  [the longest x1 3.51 us: beams(): pl.pallas_call(beams_kernel, in_specs=[pl.BlockSpec(memory_space=pltpu.VM...]
  transfers between devices with their start and end apart: 2 -> 1, of which waited for: 1 -> 0; matrix products, arithmetic and copies ran while one was open for 0% -> 0% of each run, Pallas kernels for 9% -> 7%
where the time goes in v4:
time: 132 us
  blocking collectives  110 us (83%)
  Pallas kernels  16.6 us (13%)
  starting transfers between devices  3.12 us (2%)
    all_to_all x1, blocking collectives, per_device(): turned = lax.all_to_all(spectra, 'chan', 0, 0, tiled=True)  82 us
    all_to_all x1, blocking collectives, per_device(): lax.all_to_all(averaged[None], 'chan', split_axis=1, concat_axis=2, tiled...  28.2 us
    pallas_call x1, Pallas kernels, channelize_late(): pl.pallas_call(late_kernel, in_specs=[pl.BlockSpec(memory_space=pl.ANY)]...  8.75 us
    pallas_call x1, Pallas kernels, beams(): pl.pallas_call(beams_kernel, in_specs=[pl.BlockSpec(memory_space=pltpu.VM...  3.51 us
    pallas_call x1, Pallas kernels, channelize_early(): pl.pallas_call(early_kernel, in_specs=[near, far, near, near, far], out_s...  3.41 us
    ppermute x1, starting transfers between devices, per_device(): lax.ppermute(rows[rows.shape[0] - rim:] - ZERO_SAMPLE, 'tm', [(i, i + 1)...  3.12 us
  transfers between devices with their start and end apart: 1, of which 0 were waited for; matrix products, arithmetic and copies ran while one was open for 0% of the time, Pallas kernels for 7%

profile of v4, /device:TPU:3, one launch (start us, length us, event | category | flops | bytes accessed | tf_op | source)
XLA Modules:
  0.0 132.0 jit_solution(4070893570064917515)
XLA Ops:
  0.0 1.1 slice_add_fusion
  1.1 3.1 %collective-permute-start = (s32[768,128]{1,0:T(8,128)S(1)}, s32[768,128]{1,0:T(8,128)S(1)}, u32[]{:S(2)}, u32[]{:S(2)}) collective-permute-start(s32[768,128]{1,0:T(8,128)S(1)} %bitcast.20), channel_id=1, source_target_pairs={{0,64},{64,128},{128,192},{192,256},{256,320},{320,384},{384,448},... | collective-permute-start | bytes 1179656 | tf_op jit(solution)/shard_map/ppermute | solution.py:411
  4.2 0.0 copy-start
  4.2 0.0 copy-start.2
  4.2 0.0 copy-start.3
  4.2 8.7 %channelize_late.1.into = bf16[64,8,16,128]{3,2,1,0:T(8,128)(2,1)S(1)} custom-call(s32[4096,128]{1,0:T(8,128)} %bitcast.17, bf16[6144,256]{1,0:T(8,128)(2,1)} %constant.15.clone.tables_in, f32[6144,128]{1,0:T(8,128)} %constant.16.clone.waves_in), custom_call_target="tpu_custom_call" | custom-call | flops 2415919104 | bytes 4194304 | tf_op jit(solution)/shard_map/channelize_late/pallas_call | solution.py:234
  13.0 0.0 copy-start.1
  13.0 0.0 copy-start.4
  13.0 0.0 copy-done
  13.0 0.0 copy-done.2
  13.0 0.0 copy-done.3
  13.1 1.0 stack_weights.1.weights_ref
  14.0 0.0 collective-permute-done.history
  14.1 0.0 copy-done.1
  14.1 0.1 copy-done.4
  14.1 3.4 %channelize_early.1 = bf16[64,8,16,128]{3,2,1,0:T(8,128)(2,1)S(1)} custom-call(s32[768,128]{1,0:T(8,128)S(1)} %collective-permute-done.history, s32[4096,128]{1,0:T(8,128)} %bitcast.18, bf16[1024,256]{1,0:T(8,128)(2,1)S(1)} %copy-done.1, f32[512,128]{1,0:T(8,128)S(1)} %copy-done.4, ...), custom_call_target="tpu_custom_call", output_to_operand_aliasing={{}: (4, {})} | custom-call | flops 805306368 | bytes 2097152 | tf_op jit(solution)/shard_map/channelize_early/pallas_call | solution.py:281
  17.5 82.0 %all_to_all.23.spectra_ref = bf16[64,8,16,128]{3,2,1,0:T(8,128)(2,1)S(1)} all-to-all(bf16[64,8,16,128]{3,2,1,0:T(8,128)(2,1)S(1)} %channelize_early.1), channel_id=1, replica_groups=mesh['tm'=8,'chan'=64] {'chan'}, dimensions={0} | all-to-all | bytes 4194304 | tf_op jit(solution)/shard_map/all_to_all | solution.py:422
  99.5 3.5 %beams.1 = f32[768,128]{1,0:T(8,128)S(1)} custom-call(bf16[1536,512]{1,0:T(8,128)(2,1)S(1)} %stack_weights.1.weights_ref, bf16[64,8,16,128]{3,2,1,0:T(8,128)(2,1)S(1)} %all_to_all.23.spectra_ref), custom_call_target="tpu_custom_call" | custom-call | flops 3221225472 | bytes 4063232 | tf_op jit(solution)/shard_map/beams/pallas_call | solution.py:388
  103.0 28.2 %all_to_all.24 = f32[1,768,128]{2,0,1:T(1,128)S(1)} all-to-all(f32[1,768,128]{2,0,1:T(1,128)S(1)} %bitcast.15), channel_id=1, replica_groups=mesh['tm'=8,'chan'=64] {'chan'}, dimensions={1} | all-to-all | bytes 786432 | tf_op jit(solution)/shard_map/all_to_all | solution.py:424
  131.2 0.8 copy.17
Async XLA Ops:
  1.1 13.0 %collective-permute-start = (s32[768,128]{1,0:T(8,128)S(1)}, s32[768,128]{1,0:T(8,128)S(1)}, u32[]{:S(2)}, u32[]{:S(2)}) collective-permute-start(s32[768,128]{1,0:T(8,128)S(1)} %bitcast.20), channel_id=1, source_target_pairs={{0,64},{64,128},{128,192},{192,256},{256,320},{320,384},{384,448},... | collective-permute-start | bytes 1179656 | tf_op jit(solution)/shard_map/ppermute | solution.py:411
  4.2 8.8 %copy-start = (s32[1,768,256]{2,1,0:T(8,128)S(1)}, s32[1,768,256]{2,1,0:T(8,128)}, u32[]{:S(2)}) copy-start(s32[1,768,256]{2,1,0:T(8,128)} %param.9) | copy-start | bytes 2359300
  4.2 8.8 %copy-start.2 = (bf16[512,512]{1,0:T(8,128)(2,1)S(1)}, bf16[512,512]{1,0:T(8,128)(2,1)}, u32[]{:S(2)}) copy-start(bf16[512,512]{1,0:T(8,128)(2,1)} %constant.18.clone.lower) | copy-start | bytes 1572868
  4.2 8.8 %copy-start.3 = (bf16[512,512]{1,0:T(8,128)(2,1)S(1)}, bf16[512,512]{1,0:T(8,128)(2,1)}, u32[]{:S(2)}) copy-start(bf16[512,512]{1,0:T(8,128)(2,1)} %constant.17.clone.upper) | copy-start | bytes 1572868
  13.0 1.1 copy-start.1
  13.0 1.1 copy-start.4

commit v5 on v4

--- a/solution.py
+++ b/solution.py
@@ -98,9 +98,9 @@
     return dot(left_high, right_high) + (dot(left_high, right_low) + dot(left_low, right_high))
 
 
-def channelize_pair(load, tables, waves, strided):
+def filtered(load, waves, inputs):
     columns = []
-    for i in range(INPUTS_HERE):
+    for i in inputs:
         summed = {}
         for t in range(TAPS + 1):
             packed = load(t, i)
@@ -118,13 +118,14 @@
         columns.append(
             jnp.concatenate([summed[f, part] for f in range(2) for part in range(2)], axis=0)
         )
-    frames = jnp.concatenate(columns, axis=1)
-    size = 4 * OUTER
-    first = careful_dot(tables[:size], tables[size : 2 * size], frames, ((1,), (0,)))
+    return jnp.concatenate(columns, axis=1)
+
+
+def twisted(first, waves, count):
     cos_part = waves[TAPS * OUTER : TAPS * OUTER + SECTION]
     sin_part = waves[TAPS * OUTER + SECTION : TAPS * OUTER + 2 * SECTION]
     turned = []
-    for i in range(INPUTS_HERE):
+    for i in range(count):
         real_part = first[:SECTION, i * SECTION : (i + 1) * SECTION]
         imag_part = first[SECTION:, i * SECTION : (i + 1) * SECTION]
         turned.append(
@@ -136,24 +137,42 @@
                 axis=1,
             )
         )
-    turned = jnp.concatenate(turned, axis=0)
-    spectra = careful_dot(
-        tables[2 * size : 3 * size], tables[3 * size : 4 * size], turned, ((1,), (1,))
-    )
+    return jnp.concatenate(turned, axis=0)
+
+
+def interleave(spectra, inputs, strided):
     for half in range(2):
         for part in range(2):
             top = (half * 2 + part) * GROUPS
-            for i in range(INPUTS_HERE):
+            for at, i in enumerate(inputs):
                 row = half * 8 + i * 2 + part
                 strided[pl.ds(row, GROUPS, stride=PAIR_ROWS), :] = spectra[
-                    top : top + GROUPS, i * SECTION : (i + 1) * SECTION
+                    top : top + GROUPS, at * SECTION : (at + 1) * SECTION
                 ]
-    return strided[...].astype(jnp.bfloat16).reshape(GROUPS, PAIR_ROWS, SECTION)
+
+
+def channelize_pairs(loads, tables, waves, strided, finish):
+    size = 4 * OUTER
+    sets = [(0, 1), (2, 3)]
+    steps = [(pair, inputs) for pair in range(len(loads)) for inputs in sets]
+    frames = filtered(loads[0], waves, sets[0])
+    for number, (pair, inputs) in enumerate(steps):
+        first = careful_dot(tables[:size], tables[size : 2 * size], frames, ((1,), (0,)))
+        if number + 1 < len(steps):
+            next_pair, next_inputs = steps[number + 1]
+            frames = filtered(loads[next_pair], waves, next_inputs)
+        turned = twisted(first, waves, len(inputs))
+        spectra = careful_dot(
+            tables[2 * size : 3 * size], tables[3 * size : 4 * size], turned, ((1,), (1,))
+        )
+        interleave(spectra, inputs, strided.at[pair])
+        if inputs == sets[-1]:
+            finish(pair, strided[pair].astype(jnp.bfloat16).reshape(GROUPS, PAIR_ROWS, SECTION))
 
 
 def late_kernel(
-    rows, tables_in, waves_in, out,
-    frames, tables, waves, strided, staged, frame_sem, table_sem, out_sem,
+    rows, tables_in, waves_in, out, head,
+    frames, tables, waves, strided, staged, frame_sem, table_sem, out_sem, head_sem,
 ):
     pairs = staged.shape[0]
     start = (2 * EARLY_PAIRS - (TAPS - 1)) * FRAME_ROWS
@@ -184,26 +203,30 @@
     def _(pair):
         fetch(pair).start()
 
+    head_copy = pltpu.make_async_copy(rows.at[pl.ds(0, head.shape[0])], head, head_sem)
+    head_copy.start()
     for copy in table_copies:
         copy.wait()
     fetch(0).wait()
 
-    @pl.loop(0, pairs)
+    @pl.loop(1, pairs)
     def _(pair):
-        @pl.when(pair > 0)
-        def _():
-            fetch(pair).wait()
-
+        fetch(pair).wait()
+
+    def loader(pair):
         def load(t, i):
-            return frames[
-                pl.ds(pair * step + t * FRAME_ROWS + i, OUTER, stride=INPUTS_HERE), :
-            ]
-
-        staged[pair] = channelize_pair(load, tables, waves, strided)
+            at = pair * step + t * FRAME_ROWS + i
+            return frames[pl.ds(at, OUTER, stride=INPUTS_HERE), :]
+
+        return load
+
+    def finish(pair, spectra):
+        staged[pair] = spectra
         send(pair).start()
 
-    @pl.loop(0, pairs)
-    def _(pair):
+    channelize_pairs([loader(pair) for pair in range(pairs)], tables, waves, strided, finish)
+    head_copy.wait()
+    for pair in range(pairs):
         send(pair).wait()
 
 
@@ -234,17 +257,21 @@
     return pl.pallas_call(
         late_kernel,
         in_specs=[pl.BlockSpec(memory_space=pl.ANY)] * 3,
-        out_specs=pl.BlockSpec(memory_space=pl.ANY),
-        out_shape=jax.ShapeDtypeStruct((GROUPS, all_pairs, PAIR_ROWS, SECTION), jnp.bfloat16),
+        out_specs=[pl.BlockSpec(memory_space=pl.ANY)] * 2,
+        out_shape=[
+            jax.ShapeDtypeStruct((GROUPS, all_pairs, PAIR_ROWS, SECTION), jnp.bfloat16),
+            jax.ShapeDtypeStruct((2 * EARLY_PAIRS * FRAME_ROWS, SECTION), rows.dtype),
+        ],
         scratch_shapes=[
             pltpu.VMEM(((2 * pairs + TAPS - 1) * FRAME_ROWS, SECTION), jnp.int32),
             pltpu.VMEM(tables.shape, tables.dtype),
             pltpu.VMEM(waves.shape, waves.dtype),
-            pltpu.VMEM((GROUPS * PAIR_ROWS, SECTION), jnp.float32),
+            pltpu.VMEM((pairs, GROUPS * PAIR_ROWS, SECTION), jnp.float32),
             pltpu.VMEM((pairs, GROUPS, PAIR_ROWS, SECTION), jnp.bfloat16),
             pltpu.SemaphoreType.DMA((pairs,)),
             pltpu.SemaphoreType.DMA((2,)),
             pltpu.SemaphoreType.DMA((pairs,)),
+            pltpu.SemaphoreType.DMA,
         ],
         compiler_params=pltpu.CompilerParams(vmem_limit_bytes=LATE_VMEM_BYTES),
         cost_estimate=channelizer_cost(pairs),
@@ -252,42 +279,43 @@
     )(rows, *padded)
 
 
-def early_kernel(
-    history, rows_in, tables, waves, into, out, rows, strided, staged, row_sem, out_sem
-):
+def early_kernel(history, rows, tables, waves, into, out, strided, staged, out_sem):
     rim = TAPS - 1
-    fetch = pltpu.make_async_copy(rows_in.at[pl.ds(0, rows.shape[0])], rows, row_sem)
-    fetch.start()
-    fetch.wait()
-    copies = []
-    for pair in range(EARLY_PAIRS):
-
-        def load(t, i, pair=pair):
+
+    def send(pair):
+        return pltpu.make_async_copy(staged.at[pair], out.at[:, pair], out_sem.at[pair])
+
+    def loader(pair):
+        def load(t, i):
             frame = 2 * pair + t - rim
             if frame < 0:
                 at = (frame + rim) * FRAME_ROWS + i
                 return history[pl.ds(at, OUTER, stride=INPUTS_HERE), :] + ZERO_SAMPLE
             return rows[pl.ds(frame * FRAME_ROWS + i, OUTER, stride=INPUTS_HERE), :]
 
-        staged[pair] = channelize_pair(load, tables, waves, strided)
-        copies.append(pltpu.make_async_copy(staged.at[pair], out.at[:, pair], out_sem.at[pair]))
-        copies[-1].start()
-    for copy in copies:
-        copy.wait()
+        return load
+
+    def finish(pair, spectra):
+        staged[pair] = spectra
+        send(pair).start()
+
+    channelize_pairs(
+        [loader(pair) for pair in range(EARLY_PAIRS)], tables, waves, strided, finish
+    )
+    for pair in range(EARLY_PAIRS):
+        send(pair).wait()
 
 
 def channelize_early(history, rows, tables, waves, into):
     near, far = pl.BlockSpec(memory_space=pltpu.VMEM), pl.BlockSpec(memory_space=pl.ANY)
     return pl.pallas_call(
         early_kernel,
-        in_specs=[near, far, near, near, far],
+        in_specs=[near, near, near, near, far],
         out_specs=far,
         out_shape=jax.ShapeDtypeStruct(into.shape, into.dtype),
         scratch_shapes=[
-            pltpu.VMEM((2 * EARLY_PAIRS * FRAME_ROWS, SECTION), jnp.int32),
-            pltpu.VMEM((GROUPS * PAIR_ROWS, SECTION), jnp.float32),
+            pltpu.VMEM((EARLY_PAIRS, GROUPS * PAIR_ROWS, SECTION), jnp.float32),
             pltpu.VMEM((EARLY_PAIRS, GROUPS, PAIR_ROWS, SECTION), jnp.bfloat16),
-            pltpu.SemaphoreType.DMA,
             pltpu.SemaphoreType.DMA((EARLY_PAIRS,)),
         ],
         input_output_aliases={4: 0},
@@ -414,10 +442,10 @@
         [(i, i + 1) for i in range(devices - 1)],
     )
     tables, waves = channelizer_tables()
-    spectra = channelize_late(rows, tables, waves, pairs)
+    spectra, head = channelize_late(rows, tables, waves, pairs)
     spectra, packed_weights = lax.optimization_barrier((spectra, beam_weights[0]))
     weights = stacked_weights(packed_weights)
-    spectra = channelize_early(history, rows, tables, waves, spectra)
+    spectra = channelize_early(history, head, tables, waves, spectra)
     spectra, weights = lax.optimization_barrier((spectra, weights))
     turned = lax.all_to_all(spectra, "chan", 0, 0, tiled=True)
     averaged = beams(weights, turned)

time: 132 us -> 131 us (level)
  no operation moved by 1% of the time
where the time goes in v5:
time: 131 us
  blocking collectives  110 us (84%)
  Pallas kernels  15.5 us (12%)
  starting transfers between devices  3.12 us (2%)
    all_to_all x1, blocking collectives, per_device(): turned = lax.all_to_all(spectra, 'chan', 0, 0, tiled=True)  82.2 us
    all_to_all x1, blocking collectives, per_device(): lax.all_to_all(averaged[None], 'chan', split_axis=1, concat_axis=2, tiled...  27.9 us
    pallas_call x1, Pallas kernels, channelize_late(): pl.pallas_call(late_kernel, in_specs=[pl.BlockSpec(memory_space=pl.ANY)]...  8.77 us
    pallas_call x1, Pallas kernels, beams(): pl.pallas_call(beams_kernel, in_specs=[pl.BlockSpec(memory_space=pltpu.VM...  3.51 us
    ppermute x1, starting transfers between devices, per_device(): lax.ppermute(rows[rows.shape[0] - rim:] - ZERO_SAMPLE, 'tm', [(i, i + 1)...  3.12 us
  transfers between devices with their start and end apart: 1, of which 0 were waited for; matrix products, arithmetic and copies ran while one was open for 0% of the time, Pallas kernels for 7%

profile of v5, /device:TPU:3, one launch (start us, length us, event | category | flops | bytes accessed | tf_op | source)
XLA Modules:
  0.0 130.8 jit_solution(9179913732165171565)
XLA Ops:
  0.0 1.1 slice_add_fusion
  1.1 3.1 %collective-permute-start = (s32[768,128]{1,0:T(8,128)S(1)}, s32[768,128]{1,0:T(8,128)S(1)}, u32[]{:S(2)}, u32[]{:S(2)}) collective-permute-start(s32[768,128]{1,0:T(8,128)S(1)} %bitcast.17), channel_id=1, source_target_pairs={{0,64},{64,128},{128,192},{192,256},{256,320},{320,384},{384,448},... | collective-permute-start | bytes 1179656 | tf_op jit(solution)/shard_map/ppermute | solution.py:439
  4.2 0.0 copy-start
  4.2 0.0 copy-start.2
  4.2 0.0 copy-start.3
  4.2 8.8 %channelize_late.1 = (bf16[64,8,16,128]{3,2,1,0:T(8,128)(2,1)S(1)}, s32[1024,128]{1,0:T(8,128)S(1)}) custom-call(s32[4096,128]{1,0:T(8,128)} %bitcast.19, bf16[6144,256]{1,0:T(8,128)(2,1)} %constant.15.clone.tables_in, f32[6144,128]{1,0:T(8,128)} %constant.16.clone.waves_in), custom_call_target="tpu_custom_call" | custom-call | flops 2415919104 | bytes 4194304 | tf_op jit(solution)/shard_map/channelize_late/pallas_call | solution.py:257
  13.0 0.0 copy-start.1
  13.0 0.0 copy-start.4
  13.0 0.0 copy-done
  13.1 0.0 copy-done.2
  13.1 0.0 copy-done.3
  13.1 1.0 stack_weights.1.weights_ref
  14.1 0.0 collective-permute-done.history
  14.1 0.0 copy-done.1
  14.1 0.1 copy-done.4
  14.1 2.3 %channelize_early.1 = bf16[64,8,16,128]{3,2,1,0:T(8,128)(2,1)S(1)} custom-call(s32[768,128]{1,0:T(8,128)S(1)} %collective-permute-done.history, s32[1024,128]{1,0:T(8,128)S(1)} %get-tuple-element.11.rows, bf16[1024,256]{1,0:T(8,128)(2,1)S(1)} %copy-done.1, f32[512,128]{1,0:T(8,128)S(1)} %copy-done.4, ...), custom_call_target="tpu_custom_call", output_to_operand_aliasing={{}: (4, {})} | custom-call | flops 805306368 | bytes 2097152 | tf_op jit(solution)/shard_map/channelize_early/pallas_call | solution.py:311
  16.4 82.2 %all_to_all.23.spectra_ref = bf16[64,8,16,128]{3,2,1,0:T(8,128)(2,1)S(1)} all-to-all(bf16[64,8,16,128]{3,2,1,0:T(8,128)(2,1)S(1)} %channelize_early.1), channel_id=1, replica_groups=mesh['tm'=8,'chan'=64] {'chan'}, dimensions={0} | all-to-all | bytes 4194304 | tf_op jit(solution)/shard_map/all_to_all | solution.py:450
  98.6 3.5 %beams.1 = f32[768,128]{1,0:T(8,128)S(1)} custom-call(bf16[1536,512]{1,0:T(8,128)(2,1)S(1)} %stack_weights.1.weights_ref, bf16[64,8,16,128]{3,2,1,0:T(8,128)(2,1)S(1)} %all_to_all.23.spectra_ref), custom_call_target="tpu_custom_call" | custom-call | flops 3221225472 | bytes 4063232 | tf_op jit(solution)/shard_map/beams/pallas_call | solution.py:416
  102.1 27.9 %all_to_all.24 = f32[1,768,128]{2,0,1:T(1,128)S(1)} all-to-all(f32[1,768,128]{2,0,1:T(1,128)S(1)} %bitcast.15), channel_id=1, replica_groups=mesh['tm'=8,'chan'=64] {'chan'}, dimensions={1} | all-to-all | bytes 786432 | tf_op jit(solution)/shard_map/all_to_all | solution.py:452
  130.0 0.8 copy.17
Async XLA Ops:
  1.1 13.0 %collective-permute-start = (s32[768,128]{1,0:T(8,128)S(1)}, s32[768,128]{1,0:T(8,128)S(1)}, u32[]{:S(2)}, u32[]{:S(2)}) collective-permute-start(s32[768,128]{1,0:T(8,128)S(1)} %bitcast.17), channel_id=1, source_target_pairs={{0,64},{64,128},{128,192},{192,256},{256,320},{320,384},{384,448},... | collective-permute-start | bytes 1179656 | tf_op jit(solution)/shard_map/ppermute | solution.py:439
  4.2 8.8 %copy-start = (s32[1,768,256]{2,1,0:T(8,128)S(1)}, s32[1,768,256]{2,1,0:T(8,128)}, u32[]{:S(2)}) copy-start(s32[1,768,256]{2,1,0:T(8,128)} %param.9) | copy-start | bytes 2359300
  4.2 8.8 %copy-start.2 = (bf16[512,512]{1,0:T(8,128)(2,1)S(1)}, bf16[512,512]{1,0:T(8,128)(2,1)}, u32[]{:S(2)}) copy-start(bf16[512,512]{1,0:T(8,128)(2,1)} %constant.18.clone.lower) | copy-start | bytes 1572868
  4.2 8.8 %copy-start.3 = (bf16[512,512]{1,0:T(8,128)(2,1)S(1)}, bf16[512,512]{1,0:T(8,128)(2,1)}, u32[]{:S(2)}) copy-start(bf16[512,512]{1,0:T(8,128)(2,1)} %constant.17.clone.upper) | copy-start | bytes 1572868
  13.0 1.1 copy-start.1
  13.0 1.1 copy-start.4

commit v6 on v5

--- a/solution.py
+++ b/solution.py
@@ -27,6 +27,12 @@
 FRAME_ROWS = OUTER * INPUTS_HERE
 PAIR_ROWS = 16
 EARLY_PAIRS = 2
+ORDER = [
+    4, 47, 59, 35, 43, 22, 6, 18, 60, 56, 24, 20, 44, 34, 63, 10,
+    7, 54, 5, 57, 33, 19, 8, 48, 13, 27, 17, 45, 62, 26, 55, 40,
+    16, 2, 37, 41, 11, 14, 46, 25, 32, 36, 21, 23, 30, 29, 53, 38,
+    3, 1, 51, 50, 61, 0, 52, 28, 49, 31, 15, 39, 9, 42, 12, 58,
+]
 
 
 def split_table(table):
@@ -71,7 +77,7 @@
 
 
 def inner_table():
-    channel = np.arange(SECTION).reshape(GROUPS, 2).T
+    channel = np.arange(SECTION).reshape(GROUPS, 2)[ORDER].T
     table = np.zeros((2, 2, GROUPS, 2, SECTION))
     for half in range(2):
         cos_part, sin_part = phasors(channel[half], np.arange(SECTION), SECTION)
@@ -172,9 +178,9 @@
 
 def late_kernel(
     rows, tables_in, waves_in, out, head,
-    frames, tables, waves, strided, staged, frame_sem, table_sem, out_sem, head_sem,
+    frames, tables, waves, strided, frame_sem, table_sem, head_sem,
 ):
-    pairs = staged.shape[0]
+    pairs = frame_sem.shape[0]
     start = (2 * EARLY_PAIRS - (TAPS - 1)) * FRAME_ROWS
     step = 2 * FRAME_ROWS
     lead = (TAPS - 1) * FRAME_ROWS
@@ -184,11 +190,6 @@
         size = lead + step if isinstance(pair, int) else step
         return pltpu.make_async_copy(
             rows.at[pl.ds(start + at, size)], frames.at[pl.ds(at, size)], frame_sem.at[pair]
-        )
-
-    def send(pair):
-        return pltpu.make_async_copy(
-            staged.at[pair], out.at[:, EARLY_PAIRS + pair], out_sem.at[pair]
         )
 
     table_copies = [
@@ -220,14 +221,15 @@
 
         return load
 
-    def finish(pair, spectra):
-        staged[pair] = spectra
-        send(pair).start()
-
-    channelize_pairs([loader(pair) for pair in range(pairs)], tables, waves, strided, finish)
+    @pl.loop(0, pairs // 3)
+    def _(turn):
+        def finish(pair, spectra):
+            out[:, EARLY_PAIRS + turn * 3 + pair] = spectra
+
+        loads = [loader(turn * 3 + pair) for pair in range(3)]
+        channelize_pairs(loads, tables, waves, strided, finish)
+
     head_copy.wait()
-    for pair in range(pairs):
-        send(pair).wait()
 
 
 def channelizer_tables():
@@ -257,7 +259,7 @@
     return pl.pallas_call(
         late_kernel,
         in_specs=[pl.BlockSpec(memory_space=pl.ANY)] * 3,
-        out_specs=[pl.BlockSpec(memory_space=pl.ANY)] * 2,
+        out_specs=[pl.BlockSpec(memory_space=pltpu.VMEM), pl.BlockSpec(memory_space=pl.ANY)],
         out_shape=[
             jax.ShapeDtypeStruct((GROUPS, all_pairs, PAIR_ROWS, SECTION), jnp.bfloat16),
             jax.ShapeDtypeStruct((2 * EARLY_PAIRS * FRAME_ROWS, SECTION), rows.dtype),
@@ -266,11 +268,9 @@
             pltpu.VMEM(((2 * pairs + TAPS - 1) * FRAME_ROWS, SECTION), jnp.int32),
             pltpu.VMEM(tables.shape, tables.dtype),
             pltpu.VMEM(waves.shape, waves.dtype),
-            pltpu.VMEM((pairs, GROUPS * PAIR_ROWS, SECTION), jnp.float32),
-            pltpu.VMEM((pairs, GROUPS, PAIR_ROWS, SECTION), jnp.bfloat16),
+            pltpu.VMEM((3, GROUPS * PAIR_ROWS, SECTION), jnp.float32),
             pltpu.SemaphoreType.DMA((pairs,)),
             pltpu.SemaphoreType.DMA((2,)),
-            pltpu.SemaphoreType.DMA((pairs,)),
             pltpu.SemaphoreType.DMA,
         ],
         compiler_params=pltpu.CompilerParams(vmem_limit_bytes=LATE_VMEM_BYTES),
@@ -279,11 +279,8 @@
     )(rows, *padded)
 
 
-def early_kernel(history, rows, tables, waves, into, out, strided, staged, out_sem):
+def early_kernel(history, rows, tables, waves, into, out, strided):
     rim = TAPS - 1
-
-    def send(pair):
-        return pltpu.make_async_copy(staged.at[pair], out.at[:, pair], out_sem.at[pair])
 
     def loader(pair):
         def load(t, i):
@@ -296,27 +293,22 @@
         return load
 
     def finish(pair, spectra):
-        staged[pair] = spectra
-        send(pair).start()
+        out[:, pair] = spectra
 
     channelize_pairs(
         [loader(pair) for pair in range(EARLY_PAIRS)], tables, waves, strided, finish
     )
-    for pair in range(EARLY_PAIRS):
-        send(pair).wait()
 
 
 def channelize_early(history, rows, tables, waves, into):
     near, far = pl.BlockSpec(memory_space=pltpu.VMEM), pl.BlockSpec(memory_space=pl.ANY)
     return pl.pallas_call(
         early_kernel,
-        in_specs=[near, near, near, near, far],
-        out_specs=far,
+        in_specs=[near, near, near, near, near],
+        out_specs=near,
         out_shape=jax.ShapeDtypeStruct(into.shape, into.dtype),
         scratch_shapes=[
             pltpu.VMEM((EARLY_PAIRS, GROUPS * PAIR_ROWS, SECTION), jnp.float32),
-            pltpu.VMEM((EARLY_PAIRS, GROUPS, PAIR_ROWS, SECTION), jnp.bfloat16),
-            pltpu.SemaphoreType.DMA((EARLY_PAIRS,)),
         ],
         input_output_aliases={4: 0},
         compiler_params=pltpu.CompilerParams(vmem_limit_bytes=EARLY_VMEM_BYTES),
@@ -328,8 +320,9 @@
 def spread_tables():
     even = np.zeros((INPUTS, INPUTS, 2))
     odd = np.zeros((INPUTS, INPUTS, 2))
-    even[np.arange(INPUTS), np.arange(INPUTS), 0] = 1.0
-    odd[np.arange(INPUTS), np.arange(INPUTS), 1] = 1.0
+    inputs = np.arange(INPUTS).reshape(GROUPS, INPUTS_HERE)[ORDER].reshape(INPUTS)
+    even[inputs, np.arange(INPUTS), 0] = 1.0
+    odd[inputs, np.arange(INPUTS), 1] = 1.0
     even = even.reshape(INPUTS, 2 * INPUTS)
     odd = odd.reshape(INPUTS, 2 * INPUTS)
     upper = np.concatenate([even, -odd], axis=0)
@@ -447,7 +440,7 @@
     weights = stacked_weights(packed_weights)
     spectra = channelize_early(history, head, tables, waves, spectra)
     spectra, weights = lax.optimization_barrier((spectra, weights))
-    turned = lax.all_to_all(spectra, "chan", 0, 0, tiled=True)
+    turned = lax.all_to_all(spectra, "chan", 0, 0, axis_index_groups=[ORDER], tiled=True)
     averaged = beams(weights, turned)
     return lax.all_to_all(averaged[None], "chan", split_axis=1, concat_axis=2, tiled=True)
 

time: 131 us -> 117 us (0.89)
  the two profiles are of different devices: /device:TPU:3 before, /device:TPU:9 now
where the time goes in v6:
time: 117 us
  blocking collectives  96.1 us (82%)
  Pallas kernels  13 us (11%)
  starting transfers between devices  3.12 us (3%)
  waiting for transfers between devices  3 us (3%)
    all_to_all x1, blocking collectives, per_device(): lax.all_to_all(spectra, 'chan', 0, 0, axis_index_groups=[ORDER], tiled=True)  69.4 us
    all_to_all x1, blocking collectives, per_device(): lax.all_to_all(averaged[None], 'chan', split_axis=1, concat_axis=2, tiled...  26.7 us
    pallas_call x1, Pallas kernels, channelize_late(): pl.pallas_call(late_kernel, in_specs=[pl.BlockSpec(memory_space=pl.ANY)]...  6.78 us
    pallas_call x1, Pallas kernels, beams(): pl.pallas_call(beams_kernel, in_specs=[pl.BlockSpec(memory_space=pltpu.VM...  3.51 us
    ppermute x1, starting transfers between devices, per_device(): lax.ppermute(rows[rows.shape[0] - rim:] - ZERO_SAMPLE, 'tm', [(i, i + 1)...  3.12 us
    ppermute x1, waiting for transfers between devices, per_device(): lax.ppermute(rows[rows.shape[0] - rim:] - ZERO_SAMPLE, 'tm', [(i, i + 1)...  3 us
  transfers between devices with their start and end apart: 1, of which 1 were waited for; matrix products, arithmetic and copies ran while one was open for 0% of the time, Pallas kernels for 7%

profile of v6, /device:TPU:9, one launch (start us, length us, event | category | flops | bytes accessed | tf_op | source)
XLA Modules:
  0.0 117.2 jit_solution(16301777305421636242)
XLA Ops:
  0.0 1.1 slice_add_fusion
  1.1 3.1 %collective-permute-start = (s32[768,128]{1,0:T(8,128)S(1)}, s32[768,128]{1,0:T(8,128)S(1)}, u32[]{:S(2)}, u32[]{:S(2)}) collective-permute-start(s32[768,128]{1,0:T(8,128)S(1)} %bitcast.17), channel_id=1, source_target_pairs={{0,64},{64,128},{128,192},{192,256},{256,320},{320,384},{384,448},... | collective-permute-start | bytes 1179656 | tf_op jit(solution)/shard_map/ppermute | solution.py:432
  4.2 0.0 copy-start
  4.2 0.0 copy-start.2
  4.2 0.0 copy-start.3
  4.2 6.8 %channelize_late.1 = (bf16[64,8,16,128]{3,2,1,0:T(8,128)(2,1)S(1)}, s32[1024,128]{1,0:T(8,128)S(1)}) custom-call(s32[4096,128]{1,0:T(8,128)} %bitcast.19, bf16[6144,256]{1,0:T(8,128)(2,1)} %constant.15.clone.tables_in, f32[6144,128]{1,0:T(8,128)} %constant.16.clone.waves_in), custom_call_target="tpu_custom_call" | custom-call | flops 2415919104 | bytes 4194304 | tf_op jit(solution)/shard_map/channelize_late/pallas_call | solution.py:259
  11.0 0.0 copy-start.1
  11.0 0.0 copy-start.4
  11.1 0.0 copy-done
  11.1 0.0 copy-done.2
  11.1 0.0 copy-done.3
  11.1 1.0 stack_weights.1.weights_ref
  12.1 3.0 %collective-permute-done.history = s32[768,128]{1,0:T(8,128)S(1)} collective-permute-done((s32[768,128]{1,0:T(8,128)S(1)}, s32[768,128]{1,0:T(8,128)S(1)}, u32[]{:S(2)}, u32[]{:S(2)}) %collective-permute-start) | collective-permute-done | bytes 393248 | tf_op jit(solution)/shard_map/ppermute | solution.py:432
  15.1 0.0 copy-done.1
  15.1 0.0 copy-done.4
  15.1 1.7 %channelize_early.1 = bf16[64,8,16,128]{3,2,1,0:T(8,128)(2,1)S(1)} custom-call(s32[768,128]{1,0:T(8,128)S(1)} %collective-permute-done.history, s32[1024,128]{1,0:T(8,128)S(1)} %get-tuple-element.11.rows, bf16[1024,256]{1,0:T(8,128)(2,1)S(1)} %copy-done.1, f32[512,128]{1,0:T(8,128)S(1)} %copy-done.4, ...), custom_call_target="tpu_custom_call", output_to_operand_aliasing={{}: (4, {})} | custom-call | flops 805306368 | bytes 2097152 | tf_op jit(solution)/shard_map/channelize_early/pallas_call | solution.py:305
  16.8 69.4 %all_to_all.23.spectra_ref = bf16[64,8,16,128]{3,2,1,0:T(8,128)(2,1)S(1)} all-to-all(bf16[64,8,16,128]{3,2,1,0:T(8,128)(2,1)S(1)} %channelize_early.1), channel_id=1, replica_groups={{4,47,59,35,43,22,6,18,60,56,24,20,44,34,63,10,7,54,5,57,33,19,8,48,13,..., dimensions={0} | all-to-all | bytes 4194304 | tf_op jit(solution)/shard_map/all_to_all | solution.py:443
  86.3 3.5 %beams.1 = f32[768,128]{1,0:T(8,128)S(1)} custom-call(bf16[1536,512]{1,0:T(8,128)(2,1)S(1)} %stack_weights.1.weights_ref, bf16[64,8,16,128]{3,2,1,0:T(8,128)(2,1)S(1)} %all_to_all.23.spectra_ref), custom_call_target="tpu_custom_call" | custom-call | flops 3221225472 | bytes 4063232 | tf_op jit(solution)/shard_map/beams/pallas_call | solution.py:409
  89.8 26.7 %all_to_all.24 = f32[1,768,128]{2,0,1:T(1,128)S(1)} all-to-all(f32[1,768,128]{2,0,1:T(1,128)S(1)} %bitcast.15), channel_id=1, replica_groups=mesh['tm'=8,'chan'=64] {'chan'}, dimensions={1} | all-to-all | bytes 786432 | tf_op jit(solution)/shard_map/all_to_all | solution.py:445
  116.5 0.8 copy.17
Async XLA Ops:
  1.1 14.0 %collective-permute-start = (s32[768,128]{1,0:T(8,128)S(1)}, s32[768,128]{1,0:T(8,128)S(1)}, u32[]{:S(2)}, u32[]{:S(2)}) collective-permute-start(s32[768,128]{1,0:T(8,128)S(1)} %bitcast.17), channel_id=1, source_target_pairs={{0,64},{64,128},{128,192},{192,256},{256,320},{320,384},{384,448},... | collective-permute-start | bytes 1179656 | tf_op jit(solution)/shard_map/ppermute | solution.py:432
  4.2 6.8 %copy-start = (s32[1,768,256]{2,1,0:T(8,128)S(1)}, s32[1,768,256]{2,1,0:T(8,128)}, u32[]{:S(2)}) copy-start(s32[1,768,256]{2,1,0:T(8,128)} %param.9) | copy-start | bytes 2359300
  4.2 6.8 %copy-start.2 = (bf16[512,512]{1,0:T(8,128)(2,1)S(1)}, bf16[512,512]{1,0:T(8,128)(2,1)}, u32[]{:S(2)}) copy-start(bf16[512,512]{1,0:T(8,128)(2,1)} %constant.18.clone.lower) | copy-start | bytes 1572868
  4.2 6.8 %copy-start.3 = (bf16[512,512]{1,0:T(8,128)(2,1)S(1)}, bf16[512,512]{1,0:T(8,128)(2,1)}, u32[]{:S(2)}) copy-start(bf16[512,512]{1,0:T(8,128)(2,1)} %constant.17.clone.upper) | copy-start | bytes 1572868
  11.0 4.0 %copy-start.1 = (bf16[1024,256]{1,0:T(8,128)(2,1)S(1)}, bf16[1024,256]{1,0:T(8,128)(2,1)}, u32[]{:S(2)}) copy-start(bf16[1024,256]{1,0:T(8,128)(2,1)} %constant.19.clone.tables) | copy-start | bytes 1572868
  11.0 4.0 %copy-start.4 = (f32[512,128]{1,0:T(8,128)S(1)}, f32[512,128]{1,0:T(8,128)}, u32[]{:S(2)}) copy-start(f32[512,128]{1,0:T(8,128)} %constant.20.clone.waves) | copy-start | bytes 786436

commit v7 on v6

--- a/solution.py
+++ b/solution.py
@@ -27,6 +27,7 @@
 FRAME_ROWS = OUTER * INPUTS_HERE
 PAIR_ROWS = 16
 EARLY_PAIRS = 2
+BEAMS_HERE = BEAMS // GROUPS
 ORDER = [
     4, 47, 59, 35, 43, 22, 6, 18, 60, 56, 24, 20, 44, 34, 63, 10,
     7, 54, 5, 57, 33, 19, 8, 48, 13, 27, 17, 45, 62, 26, 55, 40,
@@ -330,8 +331,12 @@
     return upper.astype(jnp.bfloat16), lower.astype(jnp.bfloat16)
 
 
-def weights_kernel(packed_ref, upper, lower, out):
-    packed = packed_ref[...]
+def weights_kernel(packed_ref, upper, lower, out, ordered):
+    for p, device in enumerate(ORDER):
+        ordered[pl.ds(BEAMS_HERE * p, BEAMS_HERE), :] = packed_ref[
+            pl.ds(BEAMS_HERE * device, BEAMS_HERE), :
+        ]
+    packed = ordered[...]
     parts = jnp.concatenate(
         [
             ((packed >> 6) - 32).astype(jnp.float32).astype(jnp.bfloat16),
@@ -354,6 +359,7 @@
         out_shape=jax.ShapeDtypeStruct((2 * BEAMS, 2 * INPUTS), jnp.bfloat16),
         in_specs=[pl.BlockSpec(memory_space=pltpu.VMEM)] * 3,
         out_specs=pl.BlockSpec(memory_space=pltpu.VMEM),
+        scratch_shapes=[pltpu.VMEM((BEAMS, INPUTS), jnp.int32)],
         compiler_params=pltpu.CompilerParams(vmem_limit_bytes=BEAM_VMEM_BYTES),
         cost_estimate=pl.CostEstimate(
             flops=2 * 2 * BEAMS * 512 * 512, bytes_accessed=5 * 2**20, transcendentals=0
@@ -363,9 +369,11 @@
 
 
 BEAM_BLOCK = 256
-
-
-def beams_kernel(weights_ref, spectra_ref, out, total):
+CODED_ROWS = 16
+SMALLEST_POWER = 2.0**-120
+
+
+def beams_kernel(weights_ref, spectra_ref, out, total, averaged, coded):
     pairs = range(spectra_ref.shape[1])
     blocks = range(0, BEAMS, BEAM_BLOCK)
 
@@ -401,7 +409,19 @@
     for half in range(2):
         part = total[:, half * SECTION : (half + 1) * SECTION]
         sums.append((part + pltpu.roll(part, OUTER, 1)) * scale)
-    out[...] = jnp.where(lane < OUTER, sums[0], sums[1])
+    averaged[...] = jnp.where(lane < OUTER, sums[0], sums[1])
+    lane = lax.broadcasted_iota(jnp.int32, (GROUPS, SECTION), 1)
+    exponents = jnp.zeros((GROUPS, SECTION), jnp.float32)
+    coded[...] = jnp.zeros_like(coded)
+    for beam in range(BEAMS_HERE):
+        power = averaged[pl.ds(beam, GROUPS, stride=BEAMS_HERE), :]
+        top = jnp.maximum(jnp.max(power, axis=1, keepdims=True), SMALLEST_POWER)
+        exponent = jnp.floor(jnp.log2(top)) + 1.0
+        steps = jnp.floor(power * jnp.exp2(-exponent) * 32768.0 + 0.5)
+        coded[pl.ds(beam, GROUPS, stride=CODED_ROWS), :] = jnp.minimum(steps, 32767.0)
+        exponents = jnp.where(lane == beam, exponent, exponents)
+    coded[pl.ds(BEAMS_HERE, GROUPS, stride=CODED_ROWS), :] = exponents
+    out[...] = coded[...].astype(jnp.int32).astype(jnp.int16).reshape(out.shape)
 
 
 def beams(weights, spectra):
@@ -410,8 +430,12 @@
         beams_kernel,
         in_specs=[pl.BlockSpec(memory_space=pltpu.VMEM)] * 2,
         out_specs=pl.BlockSpec(memory_space=pltpu.VMEM),
-        out_shape=jax.ShapeDtypeStruct((BEAMS, SECTION), jnp.float32),
-        scratch_shapes=[pltpu.VMEM((BEAMS, 2 * SECTION), jnp.float32)],
+        out_shape=jax.ShapeDtypeStruct((GROUPS, CODED_ROWS, SECTION), jnp.int16),
+        scratch_shapes=[
+            pltpu.VMEM((BEAMS, 2 * SECTION), jnp.float32),
+            pltpu.VMEM((BEAMS, SECTION), jnp.float32),
+            pltpu.VMEM((GROUPS * CODED_ROWS, SECTION), jnp.float32),
+        ],
         compiler_params=pltpu.CompilerParams(vmem_limit_bytes=BEAM_VMEM_BYTES),
         cost_estimate=pl.CostEstimate(
             flops=pairs * 2 * 1536 * 512 * 256,
@@ -420,6 +444,31 @@
         ),
         name="beams",
     )(weights, spectra)
+
+
+def decode_kernel(coded_ref, out, values):
+    values[...] = coded_ref[...].astype(jnp.int32).astype(jnp.float32).reshape(values.shape)
+    exponents = values[pl.ds(BEAMS_HERE, GROUPS, stride=CODED_ROWS), :]
+    for beam in range(BEAMS_HERE):
+        scale = jnp.exp2(exponents[:, beam : beam + 1]) * 2.0**-15
+        rows = pl.ds(beam, GROUPS, stride=CODED_ROWS)
+        values[rows, :] = values[rows, :] * scale
+    for p, device in enumerate(ORDER):
+        out[pl.ds(device, BEAMS_HERE, stride=GROUPS), :] = values[
+            pl.ds(CODED_ROWS * p, BEAMS_HERE), :
+        ]
+
+
+def decode(coded):
+    return pl.pallas_call(
+        decode_kernel,
+        in_specs=[pl.BlockSpec(memory_space=pltpu.VMEM)],
+        out_specs=pl.BlockSpec(memory_space=pltpu.VMEM),
+        out_shape=jax.ShapeDtypeStruct((BEAMS_HERE * GROUPS, SECTION), jnp.float32),
+        scratch_shapes=[pltpu.VMEM((GROUPS * CODED_ROWS, SECTION), jnp.float32)],
+        compiler_params=pltpu.CompilerParams(vmem_limit_bytes=BEAM_VMEM_BYTES),
+        name="decode",
+    )(coded)
 
 
 def per_device(voltages, beam_weights):
@@ -441,8 +490,9 @@
     spectra = channelize_early(history, head, tables, waves, spectra)
     spectra, weights = lax.optimization_barrier((spectra, weights))
     turned = lax.all_to_all(spectra, "chan", 0, 0, axis_index_groups=[ORDER], tiled=True)
-    averaged = beams(weights, turned)
-    return lax.all_to_all(averaged[None], "chan", split_axis=1, concat_axis=2, tiled=True)
+    coded = beams(weights, turned)
+    received = lax.all_to_all(coded, "chan", 0, 0, axis_index_groups=[ORDER], tiled=True)
+    return decode(received).reshape(1, BEAMS_HERE, CHANNELS)
 
 
 def solution(mesh):

time: 117 us -> 115 us (0.983)
  blocking collectives: 96.1 us -> 92.4 us
  Pallas kernels: 13 us -> 14.6 us
    all_to_all x1, blocking collectives: 26.7 us -> 23 us  [per_device(): lax.all_to_all(coded, 'chan', 0, 0, axis_index_groups=[ORDER], tiled=True)]
    pallas_call x0 -> x1, Pallas kernels: none -> 1.31 us  [decode(): pl.pallas_call(decode_kernel, in_specs=[pl.BlockSpec(memory_space=pltpu.V...]
where the time goes in v7:
time: 115 us; the launch traced here: 114 us
  blocking collectives  92.4 us (80%)
  Pallas kernels  14.6 us (13%)
  starting transfers between devices  3.12 us (3%)
  waiting for transfers between devices  2.98 us (3%)
    all_to_all x1, blocking collectives, per_device(): lax.all_to_all(spectra, 'chan', 0, 0, axis_index_groups=[ORDER], tiled=True)  69.4 us
    all_to_all x1, blocking collectives, per_device(): lax.all_to_all(coded, 'chan', 0, 0, axis_index_groups=[ORDER], tiled=True)  23 us
    pallas_call x1, Pallas kernels, channelize_late(): pl.pallas_call(late_kernel, in_specs=[pl.BlockSpec(memory_space=pl.ANY)]...  6.78 us
    pallas_call x1, Pallas kernels, beams(): pl.pallas_call(beams_kernel, in_specs=[pl.BlockSpec(memory_space=pltpu.VM...  3.79 us
    ppermute x1, starting transfers between devices, per_device(): lax.ppermute(rows[rows.shape[0] - rim:] - ZERO_SAMPLE, 'tm', [(i, i + 1)...  3.12 us
    ppermute x1, waiting for transfers between devices, per_device(): lax.ppermute(rows[rows.shape[0] - rim:] - ZERO_SAMPLE, 'tm', [(i, i + 1)...  2.98 us
  transfers between devices with their start and end apart: 1, of which 1 were waited for; matrix products, arithmetic and copies ran while one was open for 0% of the time, Pallas kernels for 7%

profile of v7, /device:TPU:9, one launch (start us, length us, event | category | flops | bytes accessed | tf_op | source)
XLA Modules:
  0.0 114.3 jit_solution(2956316963596397421)
XLA Ops:
  0.0 1.1 slice_add_fusion
  1.1 3.1 %collective-permute-start = (s32[768,128]{1,0:T(8,128)S(1)}, s32[768,128]{1,0:T(8,128)S(1)}, u32[]{:S(2)}, u32[]{:S(2)}) collective-permute-start(s32[768,128]{1,0:T(8,128)S(1)} %bitcast.9), channel_id=1, source_target_pairs={{0,64},{64,128},{128,192},{192,256},{256,320},{320,384},{384,448},... | collective-permute-start | bytes 1179656 | tf_op jit(solution)/shard_map/ppermute | solution.py:481
  4.2 0.0 copy-start
  4.2 0.0 copy-start.2
  4.2 0.0 copy-start.3
  4.2 6.8 %channelize_late.1 = (bf16[64,8,16,128]{3,2,1,0:T(8,128)(2,1)S(1)}, s32[1024,128]{1,0:T(8,128)S(1)}) custom-call(s32[4096,128]{1,0:T(8,128)} %bitcast.11, bf16[6144,256]{1,0:T(8,128)(2,1)} %constant.15.clone.tables_in, f32[6144,128]{1,0:T(8,128)} %constant.16.clone.waves_in), custom_call_target="tpu_custom_call" | custom-call | flops 2415919104 | bytes 4194304 | tf_op jit(solution)/shard_map/channelize_late/pallas_call | solution.py:260
  11.0 0.0 copy-start.1
  11.0 0.0 copy-start.4
  11.1 0.0 copy-done
  11.1 0.0 copy-done.2
  11.1 0.0 copy-done.3
  11.1 1.0 stack_weights.1.weights_ref
  12.1 3.0 %collective-permute-done.history = s32[768,128]{1,0:T(8,128)S(1)} collective-permute-done((s32[768,128]{1,0:T(8,128)S(1)}, s32[768,128]{1,0:T(8,128)S(1)}, u32[]{:S(2)}, u32[]{:S(2)}) %collective-permute-start) | collective-permute-done | bytes 393248 | tf_op jit(solution)/shard_map/ppermute | solution.py:481
  15.1 0.0 copy-done.1
  15.1 0.0 copy-done.4
  15.1 1.7 %channelize_early.1 = bf16[64,8,16,128]{3,2,1,0:T(8,128)(2,1)S(1)} custom-call(s32[768,128]{1,0:T(8,128)S(1)} %collective-permute-done.history, s32[1024,128]{1,0:T(8,128)S(1)} %get-tuple-element.11.rows, bf16[1024,256]{1,0:T(8,128)(2,1)S(1)} %copy-done.1, f32[512,128]{1,0:T(8,128)S(1)} %copy-done.4, ...), custom_call_target="tpu_custom_call", output_to_operand_aliasing={{}: (4, {})} | custom-call | flops 805306368 | bytes 2097152 | tf_op jit(solution)/shard_map/channelize_early/pallas_call | solution.py:306
  16.8 69.4 %all_to_all.10.spectra_ref = bf16[64,8,16,128]{3,2,1,0:T(8,128)(2,1)S(1)} all-to-all(bf16[64,8,16,128]{3,2,1,0:T(8,128)(2,1)S(1)} %channelize_early.1), channel_id=1, replica_groups={{4,47,59,35,43,22,6,18,60,56,24,20,44,34,63,10,7,54,5,57,33,19,8,48,13,..., dimensions={0} | all-to-all | bytes 4194304 | tf_op jit(solution)/shard_map/all_to_all | solution.py:492
  86.3 3.8 %beams.1 = s16[64,16,128]{2,1,0:T(8,128)(2,1)S(1)} custom-call(bf16[1536,512]{1,0:T(8,128)(2,1)S(1)} %stack_weights.1.weights_ref, bf16[64,8,16,128]{3,2,1,0:T(8,128)(2,1)S(1)} %all_to_all.10.spectra_ref), custom_call_target="tpu_custom_call" | custom-call | flops 3221225472 | bytes 4063232 | tf_op jit(solution)/shard_map/beams/pallas_call | solution.py:429
  90.0 23.0 %all_to_all.11.coded_ref = s16[64,16,128]{2,1,0:T(8,128)(2,1)S(1)} all-to-all(s16[64,16,128]{2,1,0:T(8,128)(2,1)S(1)} %beams.1), channel_id=1, replica_groups={{4,47,59,35,43,22,6,18,60,56,24,20,44,34,63,10,7,54,5,57,33,19,8,48,13,..., dimensions={0} | all-to-all | bytes 524288 | tf_op jit(solution)/shard_map/all_to_all | solution.py:494
  113.0 1.3 %decode.1 = f32[768,128]{1,0:T(8,128)} custom-call(s16[64,16,128]{2,1,0:T(8,128)(2,1)S(1)} %all_to_all.11.coded_ref), custom_call_target="tpu_custom_call" | custom-call | tf_op jit(solution)/shard_map/decode/pallas_call | solution.py:463
Async XLA Ops:
  1.1 14.0 %collective-permute-start = (s32[768,128]{1,0:T(8,128)S(1)}, s32[768,128]{1,0:T(8,128)S(1)}, u32[]{:S(2)}, u32[]{:S(2)}) collective-permute-start(s32[768,128]{1,0:T(8,128)S(1)} %bitcast.9), channel_id=1, source_target_pairs={{0,64},{64,128},{128,192},{192,256},{256,320},{320,384},{384,448},... | collective-permute-start | bytes 1179656 | tf_op jit(solution)/shard_map/ppermute | solution.py:481
  4.2 6.8 %copy-start = (s32[1,768,256]{2,1,0:T(8,128)S(1)}, s32[1,768,256]{2,1,0:T(8,128)}, u32[]{:S(2)}) copy-start(s32[1,768,256]{2,1,0:T(8,128)} %param.9) | copy-start | bytes 2359300
  4.2 6.8 %copy-start.2 = (bf16[512,512]{1,0:T(8,128)(2,1)S(1)}, bf16[512,512]{1,0:T(8,128)(2,1)}, u32[]{:S(2)}) copy-start(bf16[512,512]{1,0:T(8,128)(2,1)} %constant.18.clone.lower) | copy-start | bytes 1572868
  4.2 6.8 %copy-start.3 = (bf16[512,512]{1,0:T(8,128)(2,1)S(1)}, bf16[512,512]{1,0:T(8,128)(2,1)}, u32[]{:S(2)}) copy-start(bf16[512,512]{1,0:T(8,128)(2,1)} %constant.17.clone.upper) | copy-start | bytes 1572868
  11.0 4.0 %copy-start.1 = (bf16[1024,256]{1,0:T(8,128)(2,1)S(1)}, bf16[1024,256]{1,0:T(8,128)(2,1)}, u32[]{:S(2)}) copy-start(bf16[1024,256]{1,0:T(8,128)(2,1)} %constant.19.clone.tables) | copy-start | bytes 1572868
  11.0 4.0 %copy-start.4 = (f32[512,128]{1,0:T(8,128)S(1)}, f32[512,128]{1,0:T(8,128)}, u32[]{:S(2)}) copy-start(f32[512,128]{1,0:T(8,128)} %constant.20.clone.waves) | copy-start | bytes 786436

commit v8 on v7

--- a/solution.py
+++ b/solution.py
@@ -28,6 +28,7 @@
 PAIR_ROWS = 16
 EARLY_PAIRS = 2
 BEAMS_HERE = BEAMS // GROUPS
+STRIDE_ROOM = 16
 ORDER = [
     4, 47, 59, 35, 43, 22, 6, 18, 60, 56, 24, 20, 44, 34, 63, 10,
     7, 54, 5, 57, 33, 19, 8, 48, 13, 27, 17, 45, 62, 26, 55, 40,
@@ -174,7 +175,8 @@
         )
         interleave(spectra, inputs, strided.at[pair])
         if inputs == sets[-1]:
-            finish(pair, strided[pair].astype(jnp.bfloat16).reshape(GROUPS, PAIR_ROWS, SECTION))
+            rows = strided[pair, : GROUPS * PAIR_ROWS].astype(jnp.bfloat16)
+            finish(pair, rows.reshape(GROUPS, PAIR_ROWS, SECTION))
 
 
 def late_kernel(
@@ -266,10 +268,10 @@
             jax.ShapeDtypeStruct((2 * EARLY_PAIRS * FRAME_ROWS, SECTION), rows.dtype),
         ],
         scratch_shapes=[
-            pltpu.VMEM(((2 * pairs + TAPS - 1) * FRAME_ROWS, SECTION), jnp.int32),
+            pltpu.VMEM(((2 * pairs + TAPS - 1) * FRAME_ROWS + STRIDE_ROOM, SECTION), jnp.int32),
             pltpu.VMEM(tables.shape, tables.dtype),
             pltpu.VMEM(waves.shape, waves.dtype),
-            pltpu.VMEM((3, GROUPS * PAIR_ROWS, SECTION), jnp.float32),
+            pltpu.VMEM((3, GROUPS * PAIR_ROWS + STRIDE_ROOM, SECTION), jnp.float32),
             pltpu.SemaphoreType.DMA((pairs,)),
             pltpu.SemaphoreType.DMA((2,)),
             pltpu.SemaphoreType.DMA,
@@ -296,6 +298,7 @@
     def finish(pair, spectra):
         out[:, pair] = spectra
 
+    out[:, EARLY_PAIRS:] = into[:, EARLY_PAIRS:]
     channelize_pairs(
         [loader(pair) for pair in range(EARLY_PAIRS)], tables, waves, strided, finish
     )
@@ -309,7 +312,7 @@
         out_specs=near,
         out_shape=jax.ShapeDtypeStruct(into.shape, into.dtype),
         scratch_shapes=[
-            pltpu.VMEM((EARLY_PAIRS, GROUPS * PAIR_ROWS, SECTION), jnp.float32),
+            pltpu.VMEM((EARLY_PAIRS, GROUPS * PAIR_ROWS + STRIDE_ROOM, SECTION), jnp.float32),
         ],
         input_output_aliases={4: 0},
         compiler_params=pltpu.CompilerParams(vmem_limit_bytes=EARLY_VMEM_BYTES),

time: 115 us -> 115 us (level)
  no operation moved by 1% of the time
where the time goes in v8:
time: 115 us; the launch traced here: 114 us
  blocking collectives  92.2 us (80%)
  Pallas kernels  14.7 us (13%)
  starting transfers between devices  3.12 us (3%)
  waiting for transfers between devices  2.97 us (3%)
    all_to_all x1, blocking collectives, per_device(): lax.all_to_all(spectra, 'chan', 0, 0, axis_index_groups=[ORDER], tiled=True)  69.6 us
    all_to_all x1, blocking collectives, per_device(): lax.all_to_all(coded, 'chan', 0, 0, axis_index_groups=[ORDER], tiled=True)  22.6 us
    pallas_call x1, Pallas kernels, channelize_late(): pl.pallas_call(late_kernel, in_specs=[pl.BlockSpec(memory_space=pl.ANY)]...  6.78 us
    pallas_call x1, Pallas kernels, beams(): pl.pallas_call(beams_kernel, in_specs=[pl.BlockSpec(memory_space=pltpu.VM...  3.79 us
    ppermute x1, starting transfers between devices, per_device(): lax.ppermute(rows[rows.shape[0] - rim:] - ZERO_SAMPLE, 'tm', [(i, i + 1)...  3.12 us
    ppermute x1, waiting for transfers between devices, per_device(): lax.ppermute(rows[rows.shape[0] - rim:] - ZERO_SAMPLE, 'tm', [(i, i + 1)...  2.97 us
  transfers between devices with their start and end apart: 1, of which 1 were waited for; matrix products, arithmetic and copies ran while one was open for 0% of the time, Pallas kernels for 7%

profile of v8, /device:TPU:9, one launch (start us, length us, event | category | flops | bytes accessed | tf_op | source)
XLA Modules:
  0.0 114.3 jit_solution(8324112784383355119)
XLA Ops:
  0.0 1.1 slice_add_fusion
  1.1 3.1 %collective-permute-start = (s32[768,128]{1,0:T(8,128)S(1)}, s32[768,128]{1,0:T(8,128)S(1)}, u32[]{:S(2)}, u32[]{:S(2)}) collective-permute-start(s32[768,128]{1,0:T(8,128)S(1)} %bitcast.9), channel_id=1, source_target_pairs={{0,64},{64,128},{128,192},{192,256},{256,320},{320,384},{384,448},... | collective-permute-start | bytes 1179656 | tf_op jit(solution)/shard_map/ppermute | solution.py:484
  4.2 0.0 copy-start
  4.2 0.0 copy-start.2
  4.2 0.0 copy-start.3
  4.2 6.8 %channelize_late.1 = (bf16[64,8,16,128]{3,2,1,0:T(8,128)(2,1)S(1)}, s32[1024,128]{1,0:T(8,128)S(1)}) custom-call(s32[4096,128]{1,0:T(8,128)} %bitcast.11, bf16[6144,256]{1,0:T(8,128)(2,1)} %constant.15.clone.tables_in, f32[6144,128]{1,0:T(8,128)} %constant.16.clone.waves_in), custom_call_target="tpu_custom_call" | custom-call | flops 2415919104 | bytes 4194304 | tf_op jit(solution)/shard_map/channelize_late/pallas_call | solution.py:262
  11.0 0.0 copy-start.1
  11.1 0.0 copy-start.4
  11.1 0.0 copy-done
  11.1 0.0 copy-done.2
  11.1 0.0 copy-done.3
  11.1 1.0 stack_weights.1.weights_ref
  12.1 3.0 %collective-permute-done.history = s32[768,128]{1,0:T(8,128)S(1)} collective-permute-done((s32[768,128]{1,0:T(8,128)S(1)}, s32[768,128]{1,0:T(8,128)S(1)}, u32[]{:S(2)}, u32[]{:S(2)}) %collective-permute-start) | collective-permute-done | bytes 393248 | tf_op jit(solution)/shard_map/ppermute | solution.py:484
  15.1 0.0 copy-done.1
  15.1 0.0 copy-done.4
  15.1 1.9 %channelize_early.1 = bf16[64,8,16,128]{3,2,1,0:T(8,128)(2,1)S(1)} custom-call(s32[768,128]{1,0:T(8,128)S(1)} %collective-permute-done.history, s32[1024,128]{1,0:T(8,128)S(1)} %get-tuple-element.11.rows, bf16[1024,256]{1,0:T(8,128)(2,1)S(1)} %copy-done.1, f32[512,128]{1,0:T(8,128)S(1)} %copy-done.4, ...), custom_call_target="tpu_custom_call", output_to_operand_aliasing={{}: (4, {})} | custom-call | flops 805306368 | bytes 2097152 | tf_op jit(solution)/shard_map/channelize_early/pallas_call | solution.py:309
  17.0 69.6 %all_to_all.10.spectra_ref = bf16[64,8,16,128]{3,2,1,0:T(8,128)(2,1)S(1)} all-to-all(bf16[64,8,16,128]{3,2,1,0:T(8,128)(2,1)S(1)} %channelize_early.1), channel_id=1, replica_groups={{4,47,59,35,43,22,6,18,60,56,24,20,44,34,63,10,7,54,5,57,33,19,8,48,13,..., dimensions={0} | all-to-all | bytes 4194304 | tf_op jit(solution)/shard_map/all_to_all | solution.py:495
  86.6 3.8 %beams.1 = s16[64,16,128]{2,1,0:T(8,128)(2,1)S(1)} custom-call(bf16[1536,512]{1,0:T(8,128)(2,1)S(1)} %stack_weights.1.weights_ref, bf16[64,8,16,128]{3,2,1,0:T(8,128)(2,1)S(1)} %all_to_all.10.spectra_ref), custom_call_target="tpu_custom_call" | custom-call | flops 3221225472 | bytes 4063232 | tf_op jit(solution)/shard_map/beams/pallas_call | solution.py:432
  90.4 22.6 %all_to_all.11.coded_ref = s16[64,16,128]{2,1,0:T(8,128)(2,1)S(1)} all-to-all(s16[64,16,128]{2,1,0:T(8,128)(2,1)S(1)} %beams.1), channel_id=1, replica_groups={{4,47,59,35,43,22,6,18,60,56,24,20,44,34,63,10,7,54,5,57,33,19,8,48,13,..., dimensions={0} | all-to-all | bytes 524288 | tf_op jit(solution)/shard_map/all_to_all | solution.py:497
  113.0 1.3 %decode.1 = f32[768,128]{1,0:T(8,128)} custom-call(s16[64,16,128]{2,1,0:T(8,128)(2,1)S(1)} %all_to_all.11.coded_ref), custom_call_target="tpu_custom_call" | custom-call | tf_op jit(solution)/shard_map/decode/pallas_call | solution.py:466
Async XLA Ops:
  1.1 14.0 %collective-permute-start = (s32[768,128]{1,0:T(8,128)S(1)}, s32[768,128]{1,0:T(8,128)S(1)}, u32[]{:S(2)}, u32[]{:S(2)}) collective-permute-start(s32[768,128]{1,0:T(8,128)S(1)} %bitcast.9), channel_id=1, source_target_pairs={{0,64},{64,128},{128,192},{192,256},{256,320},{320,384},{384,448},... | collective-permute-start | bytes 1179656 | tf_op jit(solution)/shard_map/ppermute | solution.py:484
  4.2 6.9 %copy-start = (s32[1,768,256]{2,1,0:T(8,128)S(1)}, s32[1,768,256]{2,1,0:T(8,128)}, u32[]{:S(2)}) copy-start(s32[1,768,256]{2,1,0:T(8,128)} %param.9) | copy-start | bytes 2359300
  4.2 6.9 %copy-start.2 = (bf16[512,512]{1,0:T(8,128)(2,1)S(1)}, bf16[512,512]{1,0:T(8,128)(2,1)}, u32[]{:S(2)}) copy-start(bf16[512,512]{1,0:T(8,128)(2,1)} %constant.18.clone.lower) | copy-start | bytes 1572868
  4.2 6.9 %copy-start.3 = (bf16[512,512]{1,0:T(8,128)(2,1)S(1)}, bf16[512,512]{1,0:T(8,128)(2,1)}, u32[]{:S(2)}) copy-start(bf16[512,512]{1,0:T(8,128)(2,1)} %constant.17.clone.upper) | copy-start | bytes 1572868
  11.0 4.0 %copy-start.1 = (bf16[1024,256]{1,0:T(8,128)(2,1)S(1)}, bf16[1024,256]{1,0:T(8,128)(2,1)}, u32[]{:S(2)}) copy-start(bf16[1024,256]{1,0:T(8,128)(2,1)} %constant.19.clone.tables) | copy-start | bytes 1572868
  11.1 4.0 %copy-start.4 = (f32[512,128]{1,0:T(8,128)S(1)}, f32[512,128]{1,0:T(8,128)}, u32[]{:S(2)}) copy-start(f32[512,128]{1,0:T(8,128)} %constant.20.clone.waves) | copy-start | bytes 786436
